TPU v7x, 32 devices: a whole 2x2x4 slice. The times are simulated.
32 devices in a mesh: shell: 8 (over z, x), blk: 4 (over y, core).
Axes of the slice: x: 2, y: 2, z: 4, core: 2. Of those that a mesh axis runs over, the one named last changes fastest.
Arguments:
- cycle_fourier: bfloat16 [512, 2, 192, 1024], P('shell', None, None, 'blk'), may hold values from -6 to 6
- legendre: bfloat16 [192, 768, 1024], P('shell', None, 'blk'), may hold values from -0.1875 to 0.1875
- azimuth_orders: int32 [192], replicated, may hold values from 0 to 767, as said below
- multipole: int32 [768], P(('shell', 'blk')), may hold values from 0 to 767, each once
- bessel: bfloat16 [768, 512, 512], P(('shell', 'blk')), may hold values from -0.25 to 0.25
- signal_power: float32 [768, 512], P(('shell', 'blk')), may hold values from 0.1 to 10
- noise_power: float32 [768, 512], P(('shell', 'blk')), may hold values from 0.1 to 10
Outputs:
- filtered: bfloat16 [768, 512, 384], P('shell', 'blk')
Inputs may be any that keep to these rules, and one draw needn't show every extreme that they name: `azimuth_orders`: distinct orders; 0 and 767 always among them. Each multipole 0 to 767 appears once.
All inputs are finite; a program needn't handle non-finite values.
Results may differ from a plain program's by a relative error of at most 0.017.
Values may be sent and summed in bfloat16 or wider, within the bound.
No kernel may reach another device: no remote copies, remote signals or barrier semaphores. Data moves between devices by JAX's collectives and lax.ppermute only.
A program may use at most 192 MiB of HBM per device.

v0:
```python
import jax
import jax.numpy as jnp
from jax import lax
from jax.sharding import PartitionSpec as P


def body(cycle_fourier, legendre, azimuth_orders, multipole, bessel, signal_power, noise_power):
    fields = lax.all_to_all(cycle_fourier, "shell", split_axis=2, concat_axis=0, tiled=True)
    shell_count = lax.axis_size("shell")
    group_count = lax.axis_size("blk")
    local_cols = legendre.shape[0]
    local_cycles = legendre.shape[2]
    local_rows = legendre.shape[1] // (shell_count * group_count)
    shaped = legendre.reshape(local_cols, shell_count, group_count, local_rows, local_cycles)
    span_rows = shell_count * local_rows
    chosen = shaped
    chosen = jnp.swapaxes(chosen, 1, 2).reshape(
        local_cols, lax.axis_size("blk") * span_rows, local_cycles
    )
    summed = lax.psum_scatter(
        jnp.einsum("jir,scjr->ijcs", chosen, fields, preferred_element_type=jnp.float32).astype(
            jnp.bfloat16
        ),
        "blk",
        scatter_dimension=0,
        tiled=True,
    )
    coeffs = lax.all_to_all(summed, "shell", split_axis=0, concat_axis=1, tiled=True)
    allowed = multipole[:, None] >= azimuth_orders[None, :]
    coeffs = jnp.where(allowed[:, :, None, None], coeffs, jnp.zeros((), jnp.bfloat16))
    forward = jnp.einsum("iks,ijcs->ijck", bessel, coeffs, preferred_element_type=jnp.float32)
    wiener = signal_power / (signal_power + noise_power)
    scaled = (forward * wiener[:, None, None, :]).astype(jnp.bfloat16)
    synthesis = jnp.einsum("iks,ijck->isjc", bessel, scaled, preferred_element_type=jnp.float32)
    synthesis = synthesis.astype(jnp.bfloat16).reshape(
        local_rows, bessel.shape[2], 2 * azimuth_orders.shape[0]
    )
    return lax.all_to_all(synthesis, "blk", split_axis=1, concat_axis=0, tiled=True)


def solution(mesh):
    return jax.shard_map(
        body,
        mesh=mesh,
        in_specs=(
            P("shell", None, None, "blk"),
            P("shell", None, "blk"),
            P(),
            P(("shell", "blk")),
            P(("shell", "blk"), None, None),
            P(("shell", "blk"), None),
            P(("shell", "blk"), None),
        ),
        out_specs=P("shell", "blk", None),
        check_vma=False,
    )
```

profile of v0, /device:TPU:0, one launch (start us, length us, event | category | flops | bytes accessed | tf_op | source)
XLA Modules:
  0.0 1053.7 jit_solution(10803295260408334280)
XLA Ops:
  6.5 14.0 %copy.32 = bf16[64,2,192,256]{3,0,1,2:T(8,128)(2,1)} copy(bf16[64,2,192,256]{3,2,1,0:T(8,128)(2,1)} %param.7) | data formatting | bytes 25165824 | tf_op args[0]
  20.6 7.3 all-to-all-start
  27.8 0.0 reduce-scatter.2.cloned.1.call-start
  27.9 8.7 copy.34
  36.6 264.3 %all-to-all-done = bf16[64,2,192,256]{3,0,1,2:T(8,128)(2,1)} async-done(((bf16[64,2,192,256]{3,0,1,2:T(8,128)(2,1)}), bf16[64,2,192,256]{3,0,1,2:T(8,128)(2,1)}, u32[]{:S(2)}, u32[]{:S(2)}) %all-to-all-start) | async-done | bytes 12582944 | tf_op jit(solution)/shard_map/all_to_all | solution.py:8
  300.9 10.7 %copy.33 = bf16[64,2,8,24,256]{4,0,2,1,3:T(8,128)(2,1)} copy(bf16[64,2,8,24,256]{4,0,1,3,2:T(8,128)(2,1)} %bitcast) | data formatting | bytes 25165824 | tf_op jit(solution)/shard_map/all_to_all | solution.py:8
  311.5 27.1 %convert_bitcast_fusion = bf16[768,24,2,512]{0,3,2,1:T(8,128)(2,1)} fusion(bf16[512,2,24,256]{3,0,1,2:T(8,128)(2,1)} %bitcast.42, bf16[24,768,256,1]{2,1,3,0:T(8,128)(2,1)} %bitcast.43), kind=kOutput, calls=%fused_computation | convolution fusion | flops 9682550784 | bytes 59768832 | tf_op jit(solution)/shard_map/jir,scjr->ijcs/dot_general | solution.py:21
  338.7 47.4 %copy.35 = bf16[768,24,2,512]{3,1,2,0:T(8,128)(2,1)} copy(bf16[768,24,2,512]{0,3,2,1:T(8,128)(2,1)} %convert_bitcast_fusion) | data formatting | bytes 75497472 | tf_op jit(solution)/shard_map/convert_element_type | solution.py:21
  386.0 0.0 reduce-scatter.2.cloned.1.call-update
  386.1 0.0 copy-start.2
  386.1 0.0 copy-start.3
  386.1 0.0 copy-start
  386.1 0.0 copy-start.1
  386.1 260.8 %reduce-scatter.2.cloned.1.call-done = bf16[192,24,2,512]{3,1,2,0:T(8,128)(2,1)} async-done(((bf16[768,24,2,512]{3,1,2,0:T(8,128)(2,1)}), bf16[192,24,2,512]{3,1,2,0:T(8,128)(2,1)}) %reduce-scatter.2.cloned.1.call-update) | async-done | bytes 9437200 | tf_op jit(solution)/shard_map/reduce_scatter | solution.py:20
  646.9 5.5 all-to-all-start.1
  652.4 0.1 broadcast_compare_fusion
  652.5 205.5 %all-to-all-done.1 = bf16[192,24,2,512]{3,1,2,0:T(8,128)(2,1)} async-done(((bf16[192,24,2,512]{3,1,2,0:T(8,128)(2,1)}), bf16[192,24,2,512]{3,1,2,0:T(8,128)(2,1)}, u32[]{:S(2)}, u32[]{:S(2)}) %all-to-all-start.1) | async-done | bytes 9437216 | tf_op jit(solution)/shard_map/all_to_all | solution.py:28
  858.0 8.8 copy.36
  866.8 9.2 bitcast_select_fusion
  875.9 22.6 %convert_bitcast_fusion.1 = bf16[24,512,192,2]{1,2,3,0:T(8,128)(2,1)} fusion(bf16[24,512,512]{2,1,0:T(8,128)(2,1)} %param.11, f32[24,512]{1,0:T(8,128)S(1)} %add_divide_fusion, bf16[24,192,2,512]{3,1,2,0:T(8,128)(2,1)} %bitcast_select_fusion), kind=kOutput, calls=%fused_computation.7 | convolution fusion | flops 9677832192 | bytes 31506432 | tf_op jit(solution)/shard_map/iks,ijck->isjc/dot_general | solution.py:34
  898.5 12.6 %copy.37 = bf16[24,512,192,2]{1,0,3,2:T(8,128)(2,1)} copy(bf16[24,512,192,2]{1,2,3,0:T(8,128)(2,1)} %convert_bitcast_fusion.1) | data formatting | bytes 18874368 | tf_op jit(solution)/shard_map/convert_element_type | solution.py:35
  911.2 13.9 %copy.38 = bf16[24,512,384]{2,0,1:T(8,128)(2,1)} copy(bf16[24,512,384]{1,0,2:T(8,128)(2,1)} %bitcast.44) | data formatting | bytes 18874368 | tf_op jit(solution)/shard_map/reshape | solution.py:35
  925.1 112.3 %all_to_all.54 = bf16[24,512,384]{2,0,1:T(8,128)(2,1)} all-to-all(bf16[24,512,384]{2,0,1:T(8,128)(2,1)} %copy.38), channel_id=1, replica_groups=mesh['shell'=8,'blk'=4] {'blk'}, dimensions={1} | all-to-all | bytes 18874368 | tf_op jit(solution)/shard_map/all_to_all | solution.py:38
  1037.4 9.4 copy.40
  (5 shorter events, 0.0 us)
Async XLA Ops:
  20.6 280.3 %all-to-all-start = ((bf16[64,2,192,256]{3,0,1,2:T(8,128)(2,1)}), bf16[64,2,192,256]{3,0,1,2:T(8,128)(2,1)}, u32[]{:S(2)}, u32[]{:S(2)}) async-start(bf16[64,2,192,256]{3,0,1,2:T(8,128)(2,1)} %copy.32), calls=%async_computation | async-start | bytes 25165824 | tf_op jit(solution)/shard_map/all_to_all | solution.py:8
  27.8 619.0 %reduce-scatter.2.cloned.1.call-start = ((), (), s32[]{:S(2)}) async-start(), calls=%async_computation.4 | async-start | bytes 47185920 | tf_op jit(solution)/shard_map/reduce_scatter | solution.py:20
  386.1 266.3 %copy-start.2 = (s32[192]{0:T(256)S(1)}, s32[192]{0:T(256)}, u32[]{:S(2)}) copy-start(s32[192]{0:T(256)} %param.9) | copy-start | bytes 2308
  386.1 266.3 %copy-start.3 = (s32[24]{0:T(128)S(1)}, s32[24]{0:T(128)}, u32[]{:S(2)}) copy-start(s32[24]{0:T(128)} %param.10) | copy-start | bytes 292
  386.1 266.4 %copy-start = (f32[24,512]{1,0:T(8,128)S(1)}, f32[24,512]{1,0:T(8,128)}, u32[]{:S(2)}) copy-start(f32[24,512]{1,0:T(8,128)} %param.12) | copy-start | bytes 147460
  386.1 266.4 %copy-start.1 = (f32[24,512]{1,0:T(8,128)S(1)}, f32[24,512]{1,0:T(8,128)}, u32[]{:S(2)}) copy-start(f32[24,512]{1,0:T(8,128)} %param.13) | copy-start | bytes 147460
  646.9 211.1 %all-to-all-start.1 = ((bf16[192,24,2,512]{3,1,2,0:T(8,128)(2,1)}), bf16[192,24,2,512]{3,1,2,0:T(8,128)(2,1)}, u32[]{:S(2)}, u32[]{:S(2)}) async-start(bf16[192,24,2,512]{3,1,2,0:T(8,128)(2,1)} %reduce-scatter.2.cloned.1.call-done), calls=%async_computation.2 | async-start | bytes 18874368 | tf_op jit(solution)/shard_map/all_to_all | solution.py:28
Sparse Core Ops, SparseCore 0:
  386.2 260.6 reduce-scatter.1
where the time goes:
time: 1060 us; the launch traced here: 1050 us
  waiting for transfers between devices  731 us (69%)
  local copies, waits for them, and re-layouts  126 us (12%)
  blocking collectives  112 us (11%)
  matrix products  49.7 us (5%)
  between operations  13.5 us (1%)
  starting transfers between devices  12.8 us (1%)
    all_to_all x1, waiting for transfers between devices, body(): lax.all_to_all(cycle_fourier, 'shell', split_axis=2, concat_axis=0, tiled...  264 us
    reduce_scatter x1, waiting for transfers between devices, body(): lax.psum_scatter(jnp.einsum('jir,scjr->ijcs', chosen, fields, preferred_e...  261 us
    all_to_all x1, waiting for transfers between devices, body(): lax.all_to_all(summed, 'shell', split_axis=0, concat_axis=1, tiled=True)  206 us
    all_to_all x1, blocking collectives, body(): lax.all_to_all(synthesis, 'blk', split_axis=1, concat_axis=0, tiled=True)  112 us
    convert_element_type x1, local copies, waits for them, and re-layouts, body(): jnp.einsum('jir,scjr->ijcs', chosen, fields, preferred_element_type=jnp.f...  47.4 us
    dot_general x1, matrix products, body(): jnp.einsum('jir,scjr->ijcs', chosen, fields, preferred_element_type=jnp.f...  27.1 us
    dot_general x1, matrix products, body(): jnp.einsum('iks,ijck->isjc', bessel, scaled, preferred_element_type=jnp.f...  22.6 us
  transfers between devices with their start and end apart: 3, of which 3 were waited for; matrix products, arithmetic and copies ran while one was open for 1% of the time, Pallas kernels for 0%

commit v1 on v0

v1 whole, which is shorter than its diff:
```python
import functools
import math

import jax
import jax.numpy as jnp
from jax import lax
from jax.experimental import pallas as pl
from jax.experimental.pallas import tpu as pltpu
from jax.sharding import PartitionSpec as P

BOTH = ("shell", "blk")
VMEM = 48 * 1024 * 1024


def exchange(blocks, axis, size):
    return [blocks[0]] + [
        lax.ppermute(blocks[d], axis, [(i, i ^ d) for i in range(size)]) for d in range(1, size)
    ]


def legendre_kernel(groups, spread, parts, me, own, *refs):
    tables, fields, out = refs[: groups - 1], refs[groups - 1], refs[groups]
    lhs = jnp.concatenate([own[0]] + [t[0] for t in tables], axis=1)
    shells = fields.shape[0]
    height = fields.shape[3] // parts
    for c in range(parts):
        rows = [
            jnp.concatenate(
                [fields[s, me[0] ^ d, 0, c * height : (c + 1) * height] for d in range(groups)], axis=1
            )
            for s in range(shells)
        ]
        rhs = jnp.concatenate(rows, axis=0)
        total = lax.dot_general(lhs, rhs, (((1,), (1,)), ((), ())), preferred_element_type=jnp.float32)
        width = shells * height
        out[:, c * width : (c + 1) * width] = total.astype(out.dtype)


def legendre_transform(me, own, tables, fields, first, count, per_device, spread, parts):
    shells, groups, _, height, cycles = fields.shape
    rows = own.shape[1]
    at, offset = first
    width = shells * height
    grid_spec = pltpu.PrefetchScalarGridSpec(
        num_scalar_prefetch=1,
        grid=(count,),
        in_specs=[
            pl.BlockSpec((1, rows, cycles), lambda u, me: (me[0] // spread * per_device + at + offset + u, 0, 0))
        ]
        + [pl.BlockSpec((1, rows, cycles), lambda u, me: (at + offset + u, 0, 0))] * (groups - 1)
        + [pl.BlockSpec((shells, groups, 1, height, cycles), lambda u, me: (0, 0, offset + u, 0, 0))],
        out_specs=pl.BlockSpec((rows, width), lambda u, me: (0, u)),
    )
    flops = 2 * count * rows * width * cycles * groups
    return pl.pallas_call(
        functools.partial(legendre_kernel, groups, spread, parts),
        grid_spec=grid_spec,
        out_shape=jax.ShapeDtypeStruct((rows, count * width), jnp.bfloat16),
        compiler_params=pltpu.CompilerParams(vmem_limit_bytes=VMEM),
        cost_estimate=pl.CostEstimate(
            flops=flops, bytes_accessed=2 * count * (rows * width + groups * cycles * (rows + width)), transcendentals=0
        ),
        name="legendre",
    )(me, own, *tables, fields)


def radial_kernel(groups, step, scalars, coeffs, orders, bessel, signal, noise, *refs):
    outs, held = refs[:groups], refs[groups]
    first = pl.program_id(0) * step
    shells, width = bessel.shape[2], held.shape[2]
    pieces = coeffs.shape[2] // shells
    for t in range(step):
        row = jnp.concatenate([coeffs[:, t, n * shells : (n + 1) * shells] for n in range(pieces)], axis=0)
        allowed = scalars[1 + first + t] >= orders[...]
        masked = jnp.where(allowed, row, jnp.zeros((), row.dtype))
        forward = lax.dot_general(bessel[t], masked, (((1,), (1,)), ((), ())), preferred_element_type=jnp.float32)
        wiener = signal[t] / (signal[t] + noise[t])
        scaled = (forward.T * wiener).astype(jnp.bfloat16)
        back = jnp.dot(scaled, bessel[t], preferred_element_type=jnp.float32).astype(jnp.bfloat16)
        for b in range(groups):
            held[b] = back[:, b * width : (b + 1) * width]
        for d in range(groups):
            outs[d][t] = held[scalars[0] ^ d]


def radial_transform(scalars, coeffs, orders, bessel, signal, noise, groups):
    devices, rows, _ = coeffs.shape
    waves, shells = bessel.shape[1:]
    columns = orders.shape[0]
    width = shells // groups
    step = 8 if rows % 8 == 0 else rows
    grid_spec = pltpu.PrefetchScalarGridSpec(
        num_scalar_prefetch=1,
        grid=(rows // step,),
        in_specs=[
            pl.BlockSpec((devices, step, coeffs.shape[2]), lambda t, s: (0, t, 0)),
            pl.BlockSpec((columns, 1), lambda t, s: (0, 0)),
            pl.BlockSpec((step, waves, shells), lambda t, s: (t, 0, 0)),
            pl.BlockSpec((step, 1, waves), lambda t, s: (t, 0, 0)),
            pl.BlockSpec((step, 1, waves), lambda t, s: (t, 0, 0)),
        ],
        out_specs=[pl.BlockSpec((step, columns, width), lambda t, s: (t, 0, 0))] * groups,
        scratch_shapes=[pltpu.VMEM((groups, columns, width), jnp.bfloat16)],
    )
    return pl.pallas_call(
        functools.partial(radial_kernel, groups, step),
        grid_spec=grid_spec,
        out_shape=[jax.ShapeDtypeStruct((rows, columns, width), jnp.bfloat16)] * groups,
        compiler_params=pltpu.CompilerParams(vmem_limit_bytes=VMEM),
        cost_estimate=pl.CostEstimate(
            flops=4 * rows * columns * waves * shells,
            bytes_accessed=2 * rows * (waves * shells + 2 * columns * shells),
            transcendentals=0,
        ),
        name="radial",
    )(scalars, coeffs, orders, bessel, signal, noise)


def order_kernel(pieces, step, me, *refs):
    ins, place, out = refs[:pieces], refs[pieces], refs[-1]
    turned = [
        jnp.concatenate([p[t].astype(jnp.float32) for p in ins], axis=0).T.astype(jnp.bfloat16) for t in range(step)
    ]
    mixed = jnp.dot(jnp.concatenate(turned, axis=0), place[...], preferred_element_type=jnp.float32)
    width = out.shape[1]
    for t in range(step):
        out[t] = mixed[t * width : (t + 1) * width].astype(out.dtype)


def put_in_order(me, pieces, place, distance, so_far, groups):
    rows, _, width = pieces[0].shape
    columns = place.shape[0]
    step = math.gcd(rows, 8)
    specs = [pl.BlockSpec((step, p.shape[1], width), lambda t, me: (t, 0, 0)) for p in pieces]
    specs.append(pl.BlockSpec((columns, columns), lambda t, me: (0, 0)))
    operands = list(pieces) + [place]
    aliases = {}
    if so_far is not None:
        specs.append(pl.BlockSpec(memory_space=pl.ANY))
        operands.append(so_far)
        aliases = {len(operands): 0}
    grid_spec = pltpu.PrefetchScalarGridSpec(
        num_scalar_prefetch=1,
        grid=(rows // step,),
        in_specs=specs,
        out_specs=pl.BlockSpec((step, width, columns), lambda t, me: ((me[0] ^ distance) * (rows // step) + t, 0, 0)),
    )
    return pl.pallas_call(
        functools.partial(order_kernel, len(pieces), step),
        grid_spec=grid_spec,
        out_shape=jax.ShapeDtypeStruct((groups * rows, width, columns), jnp.bfloat16),
        input_output_aliases=aliases,
        compiler_params=pltpu.CompilerParams(vmem_limit_bytes=VMEM),
        cost_estimate=pl.CostEstimate(
            flops=2 * rows * width * columns * columns, bytes_accessed=4 * rows * width * columns, transcendentals=0
        ),
        name="in_order",
    )(me, *operands)


def body(cycle_fourier, legendre, azimuth_orders, multipole, bessel, signal_power, noise_power):
    shells, groups = lax.axis_size("shell"), lax.axis_size("blk")
    devices = shells * groups
    here, complex_parts, orders, cycles = cycle_fourier.shape
    local_orders, rows, _ = legendre.shape
    local_rows = multipole.shape[0]
    sharers = math.gcd(local_orders, groups)
    spread = groups // sharers
    per_device = local_orders // sharers
    parts = complex_parts // spread
    all_shells = shells * here
    me = lax.axis_index("blk").astype(jnp.int32)
    me1 = me.reshape(1)

    mine = legendre.reshape(sharers, per_device, rows, cycles)
    tables = exchange(
        [None] + [lax.dynamic_index_in_dim(mine, (me ^ d) // spread, 0, False) for d in range(1, groups)], "blk", groups
    )[1:]

    half = max(per_device // 2, 1)
    spans = [(0, half), (half, per_device)]
    view = cycle_fourier.reshape(here, spread, parts, shells, sharers, per_device, cycles)

    def send_fields(lo, hi):
        packed = view[..., lo:hi, :].transpose(3, 4, 1, 5, 2, 0, 6).reshape(devices, hi - lo, parts * here, cycles)
        return packed

    def move(x):
        return lax.all_to_all(x, BOTH, split_axis=0, concat_axis=0, tiled=True)

    def received(x):
        return x.reshape(shells, groups, x.shape[1], parts * here, cycles)

    fields = [received(move(send_fields(*spans[0])))]
    late_half, *tables = lax.optimization_barrier((send_fields(*spans[1]), *tables))
    fields.append(received(move(late_half)))

    chunks = [(0, 0, half)]
    rest = per_device - half
    late = max(rest // 3, 1)
    chunks += [(1, 0, rest - late), (1, rest - late, rest)]
    chunks = [c for c in chunks if c[2] > c[1]]
    signal = signal_power[:, None, :]
    noise = noise_power[:, None, :]
    scalars = jnp.concatenate([me1, multipole])
    order_view = azimuth_orders.reshape(shells, sharers, 1, per_device, 1)
    column_view = jnp.arange(orders * complex_parts).reshape(shells, sharers, per_device, spread, parts)

    def coefficients(chunk):
        which, lo, hi = chunk
        return legendre_transform(
            me1, legendre, tables, fields[which], (spans[which][0], lo), hi - lo, per_device, spread, parts
        ).reshape(devices, local_rows, -1)

    def filtered(chunk, y):
        which, lo, hi = chunk
        first, count = spans[which][0] + lo, hi - lo
        limit = jnp.broadcast_to(
            order_view[:, :, :, first : first + count], (shells, sharers, spread, count, parts)
        ).transpose(3, 4, 0, 1, 2)
        columns = column_view[:, :, first : first + count].transpose(2, 4, 0, 1, 3)
        outs = radial_transform(scalars, y, limit.reshape(-1, 1), bessel, signal, noise, groups)
        return outs, columns.reshape(-1)

    gathered, places = [], []
    first, fields[1] = lax.optimization_barrier((coefficients(chunks[0]), fields[1]))
    arrived = move(first)
    for k in range(len(chunks)):
        if k + 1 < len(chunks):
            following = coefficients(chunks[k + 1])
            if k > 0:
                following, gathered[k - 1] = lax.optimization_barrier((following, gathered[k - 1]))
            following, arrived = lax.optimization_barrier((following, arrived))
            coming = move(following)
        outs, columns = filtered(chunks[k], arrived)
        gathered.append(outs)
        places.append(columns)
        if k + 1 < len(chunks):
            arrived = coming
    gathered = [exchange(outs, "blk", groups) for outs in gathered]
    place = (jnp.concatenate(places)[:, None] == jnp.arange(orders * complex_parts)[None, :]).astype(jnp.bfloat16)
    out = None
    for d in range(groups):
        out = put_in_order(me1, [g[d] for g in gathered], place, d, out, groups)
    return out


def solution(mesh):
    return jax.shard_map(
        body,
        mesh=mesh,
        in_specs=(
            P("shell", None, None, "blk"),
            P("shell", None, "blk"),
            P(),
            P(("shell", "blk")),
            P(("shell", "blk"), None, None),
            P(("shell", "blk"), None),
            P(("shell", "blk"), None),
        ),
        out_specs=P("shell", "blk", None),
        check_vma=False,
    )
```

time: 1060 us -> 666 us (0.63)
  waiting for transfers between devices: 731 us -> 483 us
  blocking collectives: 112 us -> 0 us
  Pallas kernels: 0 us -> 90.7 us
  local copies, waits for them, and re-layouts: 126 us -> 53.5 us
  matrix products: 49.7 us -> 0 us
  starting transfers between devices: 12.8 us -> 37.3 us
  between operations: 13.5 us -> 0.37 us
    reduce_scatter x1 -> x0, waiting for transfers between devices: 261 us -> none  [body(): lax.psum_scatter(jnp.einsum('jir,scjr->ijcs', chosen, fields, preferred_e...]
    ppermute x0 -> x12, waiting for transfers between devices: none -> 203 us  [exchange(): lax.ppermute(blocks[d], axis, [(i, i ^ d) for i in range(size)])]
    all_to_all x2 -> x5, waiting for transfers between devices: 470 us -> 280 us  [move(): return lax.all_to_all(x, BOTH, split_axis=0, concat_axis=0, tiled=True)]
    all_to_all x1 -> x0, blocking collectives: 112 us -> none  [body(): lax.all_to_all(synthesis, 'blk', split_axis=1, concat_axis=0, tiled=True)]
    pallas_call x0 -> x10, Pallas kernels: none -> 90.7 us  [the longest x3 54 us: radial_transform(): pl.pallas_call(functools.partial(radial_kernel, groups, step), grid_spec=...]
    convert_element_type x2 -> x0, local copies, waits for them, and re-layouts: 60 us -> none  [the longest x1 47.4 us: body(): jnp.einsum('jir,scjr->ijcs', chosen, fields, preferred_element_type=jnp.f...]
    dot_general x2 -> x0, matrix products: 49.7 us -> none  [the longest x1 27.1 us: body(): jnp.einsum('jir,scjr->ijcs', chosen, fields, preferred_element_type=jnp.f...]
    all_to_all x3 -> x0, local copies, waits for them, and re-layouts: 28.8 us -> none  [the longest x1 10.7 us: body(): lax.all_to_all(cycle_fourier, 'shell', split_axis=2, concat_axis=0, tiled...]
  transfers between devices with their start and end apart: 3 -> 17, of which waited for: 3 -> 8; matrix products, arithmetic and copies ran while one was open for 1% -> 2% of each run, Pallas kernels for 0% -> 13%
where the time goes in v1:
time: 666 us; the launch traced here: 665 us
  waiting for transfers between devices  483 us (73%)
  Pallas kernels  90.7 us (14%)
  local copies, waits for them, and re-layouts  53.5 us (8%)
  starting transfers between devices  37.3 us (6%)
    all_to_all x5, waiting for transfers between devices, move(): return lax.all_to_all(x, BOTH, split_axis=0, concat_axis=0, tiled=True)  280 us
    ppermute x12, waiting for transfers between devices, exchange(): lax.ppermute(blocks[d], axis, [(i, i ^ d) for i in range(size)])  203 us
    pallas_call x3, Pallas kernels, radial_transform(): pl.pallas_call(functools.partial(radial_kernel, groups, step), grid_spec=...  54 us
    unnamed x59, local copies, waits for them, and re-layouts  30.7 us
    all_to_all x5, starting transfers between devices, move(): return lax.all_to_all(x, BOTH, split_axis=0, concat_axis=0, tiled=True)  28.3 us
    pallas_call x3, Pallas kernels, legendre_transform(): pl.pallas_call(functools.partial(legendre_kernel, groups, spread, parts),...  19.6 us
    pallas_call x4, Pallas kernels, put_in_order(): pl.pallas_call(functools.partial(order_kernel, len(pieces), step), grid_s...  17.1 us
  transfers between devices with their start and end apart: 17, of which 8 were waited for; matrix products, arithmetic and copies ran while one was open for 2% of the time, Pallas kernels for 13%

profile of v1, /device:TPU:0, one launch (start us, length us, event | category | flops | bytes accessed | tf_op | source)
XLA Modules:
  0.0 665.1 jit_solution(6603430794679235646)
XLA Ops:
  0.0 11.9 %copy.28 = bf16[64,2,192,256]{3,0,2,1:T(8,128)(2,1)S(1)} copy(bf16[64,2,192,256]{3,2,1,0:T(8,128)(2,1)} %param.7) | data formatting | bytes 25165824 | tf_op args[0]
  18.6 7.4 %all-to-all-start = ((bf16[32,3,128,256]{3,2,1,0:T(8,128)(2,1)}), bf16[32,3,128,256]{3,2,1,0:T(8,128)(2,1)}, u32[]{:S(2)}, u32[]{:S(2)}) async-start(bf16[32,3,128,256]{3,2,1,0:T(8,128)(2,1)} %bitcast.58), calls=%async_computation | async-start | bytes 12582912 | tf_op jit(solution)/shard_map/all_to_all | solution.py:189
  31.6 6.5 copy.29
  38.1 102.8 %collective-permute-done.1.refs_1_ = bf16[6,768,256]{2,1,0:T(8,128)(2,1)S(1)} collective-permute-done((bf16[6,768,256]{2,1,0:T(8,128)(2,1)S(1)}, bf16[6,768,256]{2,1,0:T(8,128)(2,1)S(1)}, u32[]{:S(2)}, u32[]{:S(2)}) %collective-permute-start.1) | collective-permute-done | bytes 2359328 | tf_op jit(solution)/shard_map/ppermute | solution.py:17
  142.4 54.6 %collective-permute-done.2.refs_2_ = bf16[6,768,256]{2,1,0:T(8,128)(2,1)} collective-permute-done((bf16[6,768,256]{2,1,0:T(8,128)(2,1)S(1)}, bf16[6,768,256]{2,1,0:T(8,128)(2,1)}, u32[]{:S(2)}, u32[]{:S(2)}) %collective-permute-start.2) | collective-permute-done | bytes 2359328 | tf_op jit(solution)/shard_map/ppermute | solution.py:17
  197.0 5.1 all-to-all-start.1
  203.8 9.1 %legendre.3 = bf16[768,3072]{1,0:T(8,128)(2,1)} custom-call(s32[1]{0:T(128)} %bitcast.me, bf16[24,768,256]{2,1,0:T(8,128)(2,1)} %own.5, bf16[6,768,256]{2,1,0:T(8,128)(2,1)S(1)} %collective-permute-done.refs_0_, bf16[6,768,256]{2,1,0:T(8,128)(2,1)S(1)} %copy-done.1, bf16[6,768,256]{2,1,0:T(8,128)(2,1)} %collective-permute-done.2.refs_2_, ...), custom_call_target="tpu_custom_call" | custom-call | flops 4831838208 | bytes 15728640 | tf_op jit(solution)/shard_map/legendre/pallas_call | solution.py:55
  212.8 129.3 %all-to-all-done.1 = bf16[32,3,128,256]{3,2,1,0:T(8,128)(2,1)} async-done(((bf16[32,3,128,256]{3,2,1,0:T(8,128)(2,1)}), bf16[32,3,128,256]{3,2,1,0:T(8,128)(2,1)}, u32[]{:S(2)}, u32[]{:S(2)}) %all-to-all-start.1) | async-done | bytes 6291488 | tf_op jit(solution)/shard_map/all_to_all | solution.py:189
  342.1 5.7 all-to-all-start.2
  349.5 6.7 %legendre.5 = bf16[768,2048]{1,0:T(8,128)(2,1)} custom-call(s32[1]{0:T(128)} %bitcast.me, bf16[24,768,256]{2,1,0:T(8,128)(2,1)} %own.5, bf16[6,768,256]{2,1,0:T(8,128)(2,1)S(1)} %collective-permute-done.refs_0_, bf16[6,768,256]{2,1,0:T(8,128)(2,1)S(1)} %copy-done.2, bf16[6,768,256]{2,1,0:T(8,128)(2,1)} %collective-permute-done.2.refs_2_, ...), custom_call_target="tpu_custom_call" | custom-call | flops 3221225472 | bytes 10485760 | tf_op jit(solution)/shard_map/legendre/pallas_call | solution.py:55
  356.2 97.3 %all-to-all-done.2.coeffs = bf16[32,24,3072]{2,1,0:T(8,128)(2,1)} async-done(((bf16[32,24,3072]{2,1,0:T(8,128)(2,1)}), bf16[32,24,3072]{2,1,0:T(8,128)(2,1)}, u32[]{:S(2)}, u32[]{:S(2)}) %all-to-all-start.2) | async-done | bytes 4718624 | tf_op jit(solution)/shard_map/all_to_all | solution.py:189
  453.6 5.3 all-to-all-start.3
  459.5 3.8 legendre.4
  464.4 19.7 %radial.3 = (bf16[24,192,128]{2,1,0:T(8,128)(2,1)S(1)}, bf16[24,192,128]{2,1,0:T(8,128)(2,1)S(1)}, bf16[24,192,128]{2,1,0:T(8,128)(2,1)S(1)}, bf16[24,192,128]{2,1,0:T(8,128)(2,1)S(1)}) custom-call(s32[25]{0:T(128)S(1)} %pad_add_fusion.1.scalars, bf16[32,24,3072]{2,1,0:T(8,128)(2,1)} %all-to-all-done.2.coeffs, s32[192,1]{1,0:T(8,128)S(1)} %reshape.168.orders, ...), custom_call_target="tpu_custom_call" | custom-call | flops 4831838208 | bytes 22020096 | tf_op jit(solution)/shard_map/radial/pallas_call | solution.py:105
  486.6 43.9 %all-to-all-done.3.coeffs = bf16[32,24,2048]{2,1,0:T(8,128)(2,1)} async-done(((bf16[32,24,2048]{2,1,0:T(8,128)(2,1)}), bf16[32,24,2048]{2,1,0:T(8,128)(2,1)}, u32[]{:S(2)}, u32[]{:S(2)}) %all-to-all-start.3) | async-done | bytes 3145760 | tf_op jit(solution)/shard_map/all_to_all | solution.py:189
  530.4 4.7 all-to-all-start.4
  537.2 17.6 %radial.4 = (bf16[24,128,128]{2,1,0:T(8,128)(2,1)S(1)}, bf16[24,128,128]{2,1,0:T(8,128)(2,1)}, bf16[24,128,128]{2,1,0:T(8,128)(2,1)S(1)}, bf16[24,128,128]{2,1,0:T(8,128)(2,1)S(1)}) custom-call(s32[25]{0:T(128)S(1)} %pad_add_fusion.1.scalars, bf16[32,24,2048]{2,1,0:T(8,128)(2,1)} %all-to-all-done.3.coeffs, s32[128,1]{1,0:T(8,128)S(1)} %reshape.169.orders, ...), custom_call_target="tpu_custom_call" | custom-call | flops 3221225472 | bytes 18874368 | tf_op jit(solution)/shard_map/radial/pallas_call | solution.py:105
  562.6 9.8 %all-to-all-done.4.coeffs = bf16[32,24,1024]{2,1,0:T(8,128)(2,1)S(1)} async-done(((bf16[32,24,1024]{2,1,0:T(8,128)(2,1)}), bf16[32,24,1024]{2,1,0:T(8,128)(2,1)S(1)}, u32[]{:S(2)}, u32[]{:S(2)}) %all-to-all-start.4) | async-done | bytes 1572896 | tf_op jit(solution)/shard_map/all_to_all | solution.py:189
  574.8 16.7 %radial.5 = (bf16[24,64,128]{2,1,0:T(8,128)(2,1)S(1)}, bf16[24,64,128]{2,1,0:T(8,128)(2,1)}, bf16[24,64,128]{2,1,0:T(8,128)(2,1)S(1)}, bf16[24,64,128]{2,1,0:T(8,128)(2,1)S(1)}) custom-call(s32[25]{0:T(128)S(1)} %pad_add_fusion.1.scalars, bf16[32,24,1024]{2,1,0:T(8,128)(2,1)S(1)} %all-to-all-done.4.coeffs, s32[64,1]{1,0:T(8,128)S(1)} %copy-done.14, ...), custom_call_target="tpu_custom_call" | custom-call | flops 1610612736 | bytes 15728640 | tf_op jit(solution)/shard_map/radial/pallas_call | solution.py:105
  605.8 4.6 in_order.5.refs_4_
  610.4 12.2 %collective-permute-done.7.refs_1_ = bf16[24,128,128]{2,1,0:T(8,128)(2,1)} collective-permute-done((bf16[24,128,128]{2,1,0:T(8,128)(2,1)}, bf16[24,128,128]{2,1,0:T(8,128)(2,1)}, u32[]{:S(2)}, u32[]{:S(2)}) %collective-permute-start.7) | collective-permute-done | bytes 786464 | tf_op jit(solution)/shard_map/ppermute | solution.py:17
  622.6 33.1 %collective-permute-done.8.refs_2_ = bf16[24,64,128]{2,1,0:T(8,128)(2,1)S(1)} collective-permute-done((bf16[24,64,128]{2,1,0:T(8,128)(2,1)}, bf16[24,64,128]{2,1,0:T(8,128)(2,1)S(1)}, u32[]{:S(2)}, u32[]{:S(2)}) %collective-permute-start.8) | collective-permute-done | bytes 393248 | tf_op jit(solution)/shard_map/ppermute | solution.py:17
  655.8 4.7 in_order.6.refs_4_
  660.5 4.6 in_order.7
  (109 shorter events, 47.6 us)
Async XLA Ops:
  18.6 178.3 %all-to-all-start = ((bf16[32,3,128,256]{3,2,1,0:T(8,128)(2,1)}), bf16[32,3,128,256]{3,2,1,0:T(8,128)(2,1)}, u32[]{:S(2)}, u32[]{:S(2)}) async-start(bf16[32,3,128,256]{3,2,1,0:T(8,128)(2,1)} %bitcast.58), calls=%async_computation | async-start | bytes 12582912 | tf_op jit(solution)/shard_map/all_to_all | solution.py:189
  29.7 8.5 %collective-permute-start = (bf16[6,768,256]{2,1,0:T(8,128)(2,1)S(1)}, bf16[6,768,256]{2,1,0:T(8,128)(2,1)S(1)}, u32[]{:S(2)}, u32[]{:S(2)}) collective-permute-start(bf16[6,768,256]{2,1,0:T(8,128)(2,1)S(1)} %get-tuple-element.63), channel_id=1, source_target_pairs={{0,1},{1,0},{2,3},{3,2},{4,5},{5,4},{6,7},{7,6},{8,9},{9,8},{10,11... | collective-permute-start | bytes 7077896 | tf_op jit(solution)/shard_map/ppermute | solution.py:17
  29.9 111.0 %collective-permute-start.1 = (bf16[6,768,256]{2,1,0:T(8,128)(2,1)S(1)}, bf16[6,768,256]{2,1,0:T(8,128)(2,1)S(1)}, u32[]{:S(2)}, u32[]{:S(2)}) collective-permute-start(bf16[6,768,256]{2,1,0:T(8,128)(2,1)S(1)} %get-tuple-element.62), channel_id=1, source_target_pairs={{0,2},{1,3},{2,0},{3,1},{4,6},{5,7},{6,4},{7,5},{8,10},{9,11},{10,... | collective-permute-start | bytes 7077896 | tf_op jit(solution)/shard_map/ppermute | solution.py:17
  31.6 165.4 %collective-permute-start.2 = (bf16[6,768,256]{2,1,0:T(8,128)(2,1)S(1)}, bf16[6,768,256]{2,1,0:T(8,128)(2,1)}, u32[]{:S(2)}, u32[]{:S(2)}) collective-permute-start(bf16[6,768,256]{2,1,0:T(8,128)(2,1)S(1)} %get-tuple-element.61), channel_id=1, source_target_pairs={{0,3},{1,2},{2,1},{3,0},{4,7},{5,6},{6,5},{7,4},{8,11},{9,10},{10,... | collective-permute-start | bytes 7077896 | tf_op jit(solution)/shard_map/ppermute | solution.py:17
  197.0 145.1 %all-to-all-start.1 = ((bf16[32,3,128,256]{3,2,1,0:T(8,128)(2,1)}), bf16[32,3,128,256]{3,2,1,0:T(8,128)(2,1)}, u32[]{:S(2)}, u32[]{:S(2)}) async-start(bf16[32,3,128,256]{3,2,1,0:T(8,128)(2,1)} %bitcast.59), calls=%async_computation.1 | async-start | bytes 12582912 | tf_op jit(solution)/shard_map/all_to_all | solution.py:189
  342.1 111.4 %all-to-all-start.2 = ((bf16[32,24,3072]{2,1,0:T(8,128)(2,1)}), bf16[32,24,3072]{2,1,0:T(8,128)(2,1)}, u32[]{:S(2)}, u32[]{:S(2)}) async-start(bf16[32,24,3072]{2,1,0:T(8,128)(2,1)} %bitcast.60), calls=%async_computation.2 | async-start | bytes 9437184 | tf_op jit(solution)/shard_map/all_to_all | solution.py:189
  356.2 102.7 %copy-start.27 = (s32[192]{0:T(256)S(1)}, s32[192]{0:T(256)}, u32[]{:S(2)}) copy-start(s32[192]{0:T(256)} %param.9) | copy-start | bytes 2308
  356.2 103.0 %copy-start.25 = (f32[24,512]{1,0:T(8,128)S(1)}, f32[24,512]{1,0:T(8,128)}, u32[]{:S(2)}) copy-start(f32[24,512]{1,0:T(8,128)} %param.12) | copy-start | bytes 147460
  356.2 103.1 %copy-start.26 = (f32[24,512]{1,0:T(8,128)S(1)}, f32[24,512]{1,0:T(8,128)}, u32[]{:S(2)}) copy-start(f32[24,512]{1,0:T(8,128)} %param.13) | copy-start | bytes 147460
  356.2 103.1 %copy-start.28 = (s32[24]{0:T(128)S(1)}, s32[24]{0:T(128)}, u32[]{:S(2)}) copy-start(s32[24]{0:T(128)} %param.10) | copy-start | bytes 292
  453.6 76.9 %all-to-all-start.3 = ((bf16[32,24,2048]{2,1,0:T(8,128)(2,1)}), bf16[32,24,2048]{2,1,0:T(8,128)(2,1)}, u32[]{:S(2)}, u32[]{:S(2)}) async-start(bf16[32,24,2048]{2,1,0:T(8,128)(2,1)} %bitcast.61), calls=%async_computation.3 | async-start | bytes 6291456 | tf_op jit(solution)/shard_map/all_to_all | solution.py:189
  459.0 77.8 %copy-start.22 = (s32[8,4,1,6,1]{3,1,0,4,2:T(4,128)}, s32[8,4,1,6,1]{3,1,0,4,2:T(4,128)S(1)}, u32[]{:S(2)}) copy-start(s32[8,4,1,6,1]{3,1,0,4,2:T(4,128)S(1)} %reshape.153) | copy-start | bytes 2308
  459.3 77.8 %copy-start.6 = (f32[24,1,512]{2,1,0:T(1,128)}, f32[24,1,512]{2,1,0:T(1,128)S(1)}, u32[]{:S(2)}) copy-start(f32[24,1,512]{2,1,0:T(1,128)S(1)} %broadcast_in_dim.29.signal) | copy-start | bytes 147460
  459.4 77.8 %copy-start.8 = (f32[24,1,512]{2,1,0:T(1,128)}, f32[24,1,512]{2,1,0:T(1,128)S(1)}, u32[]{:S(2)}) copy-start(f32[24,1,512]{2,1,0:T(1,128)S(1)} %broadcast_in_dim.30.noise) | copy-start | bytes 147460
  530.4 42.0 %all-to-all-start.4 = ((bf16[32,24,1024]{2,1,0:T(8,128)(2,1)}), bf16[32,24,1024]{2,1,0:T(8,128)(2,1)S(1)}, u32[]{:S(2)}, u32[]{:S(2)}) async-start(bf16[32,24,1024]{2,1,0:T(8,128)(2,1)} %bitcast.55), calls=%async_computation.4 | async-start | bytes 3145728 | tf_op jit(solution)/shard_map/all_to_all | solution.py:189
  535.2 58.7 %collective-permute-start.6 = (bf16[24,192,128]{2,1,0:T(8,128)(2,1)}, bf16[24,192,128]{2,1,0:T(8,128)(2,1)}, u32[]{:S(2)}, u32[]{:S(2)}) collective-permute-start(bf16[24,192,128]{2,1,0:T(8,128)(2,1)} %copy-done.17), channel_id=1, source_target_pairs={{0,2},{1,3},{2,0},{3,1},{4,6},{5,7},{6,4},{7,5},{8,10},{9,11},{10,... | collective-permute-start | bytes 3538952 | tf_op jit(solution)/shard_map/ppermute | solution.py:17
  537.0 58.5 %collective-permute-start.9 = (bf16[24,192,128]{2,1,0:T(8,128)(2,1)}, bf16[24,192,128]{2,1,0:T(8,128)(2,1)}, u32[]{:S(2)}, u32[]{:S(2)}) collective-permute-start(bf16[24,192,128]{2,1,0:T(8,128)(2,1)} %copy-done.16), channel_id=1, source_target_pairs={{0,1},{1,0},{2,3},{3,2},{4,5},{5,4},{6,7},{7,6},{8,9},{9,8},{10,11... | collective-permute-start | bytes 3538952 | tf_op jit(solution)/shard_map/ppermute | solution.py:17
  557.6 40.4 %collective-permute-start.10 = (bf16[24,128,128]{2,1,0:T(8,128)(2,1)}, bf16[24,128,128]{2,1,0:T(8,128)(2,1)S(1)}, u32[]{:S(2)}, u32[]{:S(2)}) collective-permute-start(bf16[24,128,128]{2,1,0:T(8,128)(2,1)} %get-tuple-element.54), channel_id=1, source_target_pairs={{0,1},{1,0},{2,3},{3,2},{4,5},{5,4},{6,7},{7,6},{8,9},{9,8},{10,11... | collective-permute-start | bytes 2359304 | tf_op jit(solution)/shard_map/ppermute | solution.py:17
  561.0 99.6 %collective-permute-start.3 = (bf16[24,192,128]{2,1,0:T(8,128)(2,1)}, bf16[24,192,128]{2,1,0:T(8,128)(2,1)}, u32[]{:S(2)}, u32[]{:S(2)}) collective-permute-start(bf16[24,192,128]{2,1,0:T(8,128)(2,1)} %copy-done.15), channel_id=1, source_target_pairs={{0,3},{1,2},{2,1},{3,0},{4,7},{5,6},{6,5},{7,4},{8,11},{9,10},{10,... | collective-permute-start | bytes 3538952 | tf_op jit(solution)/shard_map/ppermute | solution.py:17
  561.1 61.6 %collective-permute-start.7 = (bf16[24,128,128]{2,1,0:T(8,128)(2,1)}, bf16[24,128,128]{2,1,0:T(8,128)(2,1)}, u32[]{:S(2)}, u32[]{:S(2)}) collective-permute-start(bf16[24,128,128]{2,1,0:T(8,128)(2,1)} %copy-done.19), channel_id=1, source_target_pairs={{0,2},{1,3},{2,0},{3,1},{4,6},{5,7},{6,4},{7,5},{8,10},{9,11},{10,... | collective-permute-start | bytes 2359304 | tf_op jit(solution)/shard_map/ppermute | solution.py:17
  593.8 4.4 collective-permute-start.11
  595.4 65.1 %collective-permute-start.4 = (bf16[24,128,128]{2,1,0:T(8,128)(2,1)}, bf16[24,128,128]{2,1,0:T(8,128)(2,1)S(1)}, u32[]{:S(2)}, u32[]{:S(2)}) collective-permute-start(bf16[24,128,128]{2,1,0:T(8,128)(2,1)} %copy-done.18), channel_id=1, source_target_pairs={{0,3},{1,2},{2,1},{3,0},{4,7},{5,6},{6,5},{7,4},{8,11},{9,10},{10,... | collective-permute-start | bytes 2359304 | tf_op jit(solution)/shard_map/ppermute | solution.py:17
  598.0 62.5 %collective-permute-start.5 = (bf16[24,64,128]{2,1,0:T(8,128)(2,1)}, bf16[24,64,128]{2,1,0:T(8,128)(2,1)S(1)}, u32[]{:S(2)}, u32[]{:S(2)}) collective-permute-start(bf16[24,64,128]{2,1,0:T(8,128)(2,1)} %copy-done.20), channel_id=1, source_target_pairs={{0,3},{1,2},{2,1},{3,0},{4,7},{5,6},{6,5},{7,4},{8,11},{9,10},{10,... | collective-permute-start | bytes 1179656 | tf_op jit(solution)/shard_map/ppermute | solution.py:17
  599.0 56.8 %collective-permute-start.8 = (bf16[24,64,128]{2,1,0:T(8,128)(2,1)}, bf16[24,64,128]{2,1,0:T(8,128)(2,1)S(1)}, u32[]{:S(2)}, u32[]{:S(2)}) collective-permute-start(bf16[24,64,128]{2,1,0:T(8,128)(2,1)} %copy-done.21), channel_id=1, source_target_pairs={{0,2},{1,3},{2,0},{3,1},{4,6},{5,7},{6,4},{7,5},{8,10},{9,11},{10,... | collective-permute-start | bytes 1179656 | tf_op jit(solution)/shard_map/ppermute | solution.py:17
  (22 other events, 65.4 us)

commit v2 on v1

v2 whole, which is shorter than its diff:
```python
import functools
import math

import jax
import jax.numpy as jnp
from jax import lax
from jax.experimental import pallas as pl
from jax.experimental.pallas import tpu as pltpu
from jax.sharding import PartitionSpec as P

BOTH = ("shell", "blk")
FIELD_SHARES = (0, 3, 6)
SHARES = (0, 1, 3, 5, 6)
VMEM = 48 * 1024 * 1024


def exchange(blocks, axis, size):
    return [blocks[0]] + [
        lax.ppermute(blocks[d], axis, [(i, i ^ d) for i in range(size)]) for d in range(1, size)
    ]


def legendre_kernel(groups, spread, parts, me, own, *refs):
    tables, fields, out = refs[: groups - 1], refs[groups - 1], refs[groups]
    lhs = jnp.concatenate([own[0]] + [t[0] for t in tables], axis=1)
    shells = fields.shape[0]
    height = fields.shape[3] // parts
    for c in range(parts):
        rows = [
            jnp.concatenate(
                [fields[s, me[0] ^ d, 0, c * height : (c + 1) * height] for d in range(groups)], axis=1
            )
            for s in range(shells)
        ]
        rhs = jnp.concatenate(rows, axis=0)
        total = lax.dot_general(lhs, rhs, (((1,), (1,)), ((), ())), preferred_element_type=jnp.float32)
        width = shells * height
        out[:, c * width : (c + 1) * width] = total.astype(out.dtype)


def legendre_transform(me, own, tables, fields, first, count, per_device, spread, parts):
    shells, groups, _, height, cycles = fields.shape
    rows = own.shape[1]
    at, offset = first
    width = shells * height
    grid_spec = pltpu.PrefetchScalarGridSpec(
        num_scalar_prefetch=1,
        grid=(count,),
        in_specs=[
            pl.BlockSpec((1, rows, cycles), lambda u, me: (me[0] // spread * per_device + at + offset + u, 0, 0))
        ]
        + [pl.BlockSpec((1, rows, cycles), lambda u, me: (offset + u, 0, 0))] * (groups - 1)
        + [pl.BlockSpec((shells, groups, 1, height, cycles), lambda u, me: (0, 0, offset + u, 0, 0))],
        out_specs=pl.BlockSpec((rows, width), lambda u, me: (0, u)),
    )
    flops = 2 * count * rows * width * cycles * groups
    return pl.pallas_call(
        functools.partial(legendre_kernel, groups, spread, parts),
        grid_spec=grid_spec,
        out_shape=jax.ShapeDtypeStruct((rows, count * width), jnp.bfloat16),
        compiler_params=pltpu.CompilerParams(vmem_limit_bytes=VMEM),
        cost_estimate=pl.CostEstimate(
            flops=flops, bytes_accessed=2 * count * (rows * width + groups * cycles * (rows + width)), transcendentals=0
        ),
        name="legendre",
    )(me, own, *tables, fields)


def filter_kernel(bessel, signal, noise, out):
    for t in range(bessel.shape[0]):
        wiener = signal[t] / (signal[t] + noise[t])
        turned = (bessel[t].astype(jnp.float32).T * wiener).astype(jnp.bfloat16)
        out[t] = jnp.dot(turned, bessel[t], preferred_element_type=jnp.float32).astype(out.dtype)


def radial_filter(bessel, signal, noise):
    rows, waves, shells = bessel.shape
    return pl.pallas_call(
        filter_kernel,
        grid=(rows,),
        in_specs=[
            pl.BlockSpec((1, waves, shells), lambda t: (t, 0, 0)),
            pl.BlockSpec((1, 1, waves), lambda t: (t, 0, 0)),
            pl.BlockSpec((1, 1, waves), lambda t: (t, 0, 0)),
        ],
        out_specs=pl.BlockSpec((1, shells, shells), lambda t: (t, 0, 0)),
        out_shape=jax.ShapeDtypeStruct((rows, shells, shells), jnp.bfloat16),
        compiler_params=pltpu.CompilerParams(vmem_limit_bytes=VMEM),
        cost_estimate=pl.CostEstimate(
            flops=2 * rows * waves * shells * shells, bytes_accessed=4 * rows * shells * waves, transcendentals=0
        ),
        name="radial_filter",
    )(bessel, signal, noise)


def radial_kernel(groups, step, at, coeffs, orders, response, *refs):
    outs, held = refs[:groups], refs[groups]
    first = pl.program_id(0) * step
    length, width = response.shape[1], held.shape[3]
    pieces = coeffs.shape[2] // length
    for t in range(step):
        row = jnp.concatenate([coeffs[:, t, n * length : (n + 1) * length] for n in range(pieces)], axis=0)
        allowed = at[1 + first + t] >= orders[...]
        masked = jnp.where(allowed, row, jnp.zeros((), row.dtype))
        back = jnp.dot(masked, response[t], preferred_element_type=jnp.float32).astype(jnp.bfloat16)
        for b in range(groups):
            held[t, b] = back[:, b * width : (b + 1) * width]
        for d in range(groups):
            outs[d][t] = held[t, at[0] ^ d]


def radial_transform(at, coeffs, orders, response, groups):
    senders, rows, lanes = coeffs.shape
    length = response.shape[1]
    columns = orders.shape[0]
    width = length // groups
    step = 8 if rows % 8 == 0 else rows
    grid_spec = pltpu.PrefetchScalarGridSpec(
        num_scalar_prefetch=1,
        grid=(rows // step,),
        in_specs=[
            pl.BlockSpec((senders, step, lanes), lambda t, at: (0, t, 0)),
            pl.BlockSpec((columns, 1), lambda t, at: (0, 0)),
            pl.BlockSpec((step, length, length), lambda t, at: (t, 0, 0)),
        ],
        out_specs=[pl.BlockSpec((step, columns, width), lambda t, at: (t, 0, 0))] * groups,
        scratch_shapes=[pltpu.VMEM((step, groups, columns, width), jnp.bfloat16)],
    )
    return pl.pallas_call(
        functools.partial(radial_kernel, groups, step),
        grid_spec=grid_spec,
        out_shape=[jax.ShapeDtypeStruct((rows, columns, width), jnp.bfloat16)] * groups,
        compiler_params=pltpu.CompilerParams(vmem_limit_bytes=VMEM),
        cost_estimate=pl.CostEstimate(
            flops=2 * rows * columns * length * length,
            bytes_accessed=2 * rows * (length * length + 2 * columns * length),
            transcendentals=0,
        ),
        name="radial",
    )(at, coeffs, orders, response)


def order_kernel(pieces, step, me, *refs):
    ins, place, out = refs[:pieces], refs[pieces], refs[-1]
    turned = [
        jnp.concatenate([p[t].astype(jnp.float32) for p in ins], axis=0).T.astype(jnp.bfloat16) for t in range(step)
    ]
    mixed = jnp.dot(jnp.concatenate(turned, axis=0), place[...], preferred_element_type=jnp.float32)
    width = out.shape[1]
    for t in range(step):
        out[t] = mixed[t * width : (t + 1) * width].astype(out.dtype)


def put_in_order(me, pieces, place, distance, so_far, groups):
    rows, _, width = pieces[0].shape
    columns = place.shape[0]
    step = math.gcd(rows, 8)
    specs = [pl.BlockSpec((step, p.shape[1], width), lambda t, me: (t, 0, 0)) for p in pieces]
    specs.append(pl.BlockSpec((columns, columns), lambda t, me: (0, 0)))
    operands = list(pieces) + [place]
    aliases = {}
    if so_far is not None:
        specs.append(pl.BlockSpec(memory_space=pl.ANY))
        operands.append(so_far)
        aliases = {len(operands): 0}
    grid_spec = pltpu.PrefetchScalarGridSpec(
        num_scalar_prefetch=1,
        grid=(rows // step,),
        in_specs=specs,
        out_specs=pl.BlockSpec((step, width, columns), lambda t, me: ((me[0] ^ distance) * (rows // step) + t, 0, 0)),
    )
    return pl.pallas_call(
        functools.partial(order_kernel, len(pieces), step),
        grid_spec=grid_spec,
        out_shape=jax.ShapeDtypeStruct((groups * rows, width, columns), jnp.bfloat16),
        input_output_aliases=aliases,
        compiler_params=pltpu.CompilerParams(vmem_limit_bytes=VMEM),
        cost_estimate=pl.CostEstimate(
            flops=2 * rows * width * columns * columns, bytes_accessed=4 * rows * width * columns, transcendentals=0
        ),
        name="in_order",
    )(me, *operands)


def body(cycle_fourier, legendre, azimuth_orders, multipole, bessel, signal_power, noise_power):
    shells, groups = lax.axis_size("shell"), lax.axis_size("blk")
    devices = shells * groups
    here, complex_parts, orders, cycles = cycle_fourier.shape
    local_orders, rows, _ = legendre.shape
    local_rows = multipole.shape[0]
    sharers = math.gcd(local_orders, groups)
    spread = groups // sharers
    per_device = local_orders // sharers
    parts = complex_parts // spread
    me = lax.axis_index("blk").astype(jnp.int32)
    at = jnp.concatenate([me.reshape(1), multipole])

    cuts = [round(per_device * share / FIELD_SHARES[-1]) for share in FIELD_SHARES]
    spans = [(lo, hi) for lo, hi in zip(cuts, cuts[1:]) if hi > lo]
    cuts = [round(per_device * share / SHARES[-1]) for share in SHARES]
    chunks = [(lo, hi) for lo, hi in zip(cuts, cuts[1:]) if hi > lo]
    view = cycle_fourier.reshape(here, spread, parts, shells, sharers, per_device, cycles)

    def packed(span):
        lo, hi = span
        return view[..., lo:hi, :].transpose(3, 4, 1, 5, 2, 0, 6).reshape(devices, hi - lo, parts * here, cycles)

    def move(x):
        return lax.all_to_all(x, BOTH, split_axis=0, concat_axis=0, tiled=True)

    def send_tables(span, earlier):
        lo, hi = span
        blocks = [
            lax.dynamic_slice_in_dim(legendre, (me ^ d) // spread * per_device + lo, hi - lo, 0) for d in range(1, groups)
        ]
        return exchange([None] + after(earlier, blocks), "blk", groups)[1:]

    def after(earlier, later):
        return lax.optimization_barrier((earlier, later))[1]

    order_view = azimuth_orders.reshape(shells, sharers, 1, per_device, 1)
    column_view = jnp.arange(orders * complex_parts).reshape(shells, sharers, per_device, spread, parts)
    limits, places = [], []
    for lo, hi in chunks:
        limit = jnp.broadcast_to(order_view[:, :, :, lo:hi], (shells, sharers, spread, hi - lo, parts))
        limits.append(limit.transpose(3, 4, 0, 1, 2).reshape(-1, 1))
        places.append(column_view[:, :, lo:hi].transpose(2, 4, 0, 1, 3).reshape(-1))
    place = (jnp.concatenate(places)[:, None] == jnp.arange(orders * complex_parts)[None, :]).astype(jnp.bfloat16)
    response = radial_filter(bessel, signal_power[:, None, :], noise_power[:, None, :])

    fields, tables = [], []
    earlier = ()
    for k, span in enumerate(spans):
        fields.append(move(after(earlier, packed(span))))
        tables.append(send_tables(span, earlier))
        earlier = (fields[k], tables[k])
        if k == 0:
            earlier, (response, limits, place) = lax.optimization_barrier((earlier, (response, limits, place)))

    def coefficients(chunk):
        lo, hi = chunk
        which = max(i for i, span in enumerate(spans) if span[0] <= lo)
        start = spans[which][0]
        source = fields[which].reshape(shells, groups, *fields[which].shape[1:])
        sent = legendre_transform(
            at, legendre, tables[which], source, (start, lo - start), hi - lo, per_device, spread, parts
        )
        return sent.reshape(devices, local_rows, -1)

    count = len(chunks)
    sent = [coefficients(c) for c in chunks]
    early = [k for k, c in enumerate(chunks) if c[0] < spans[0][1]]
    outs, gathered = [], []
    coming = move(after(([sent[k] for k in early], fields[-1], tables), sent[0]))
    for k in range(count):
        arrived = coming
        if k + 1 < count:
            before = [arrived, sent]
            if k >= 1:
                before += [gathered[k - 1]]
            coming = move(after(before, sent[k + 1]))
        elif k >= 1:
            arrived = after((outs[k - 1], gathered[: k - 1]), arrived)
        outs.append(radial_transform(at, arrived, limits[k], response, groups))
        gathered.append(exchange(outs[k], "blk", groups))

    out = None
    for d in range(groups):
        out = put_in_order(at, [g[d] for g in gathered], place, d, out, groups)
    return out


def solution(mesh):
    return jax.shard_map(
        body,
        mesh=mesh,
        in_specs=(
            P("shell", None, None, "blk"),
            P("shell", None, "blk"),
            P(),
            P(("shell", "blk")),
            P(("shell", "blk"), None, None),
            P(("shell", "blk"), None),
            P(("shell", "blk"), None),
        ),
        out_specs=P("shell", "blk", None),
        check_vma=False,
    )
```

time: 666 us -> 590 us (0.89)
  waiting for transfers between devices: 483 us -> 398 us
  Pallas kernels: 90.7 us -> 102 us
  local copies, waits for them, and re-layouts: 53.5 us -> 44.7 us
    all_to_all x5 -> x6, waiting for transfers between devices: 280 us -> 122 us  [move(): return lax.all_to_all(x, BOTH, split_axis=0, concat_axis=0, tiled=True)]
    ppermute x12 -> x18, waiting for transfers between devices: 203 us -> 276 us  [exchange(): lax.ppermute(blocks[d], axis, [(i, i ^ d) for i in range(size)])]
    pallas_call x0 -> x1, Pallas kernels: none -> 22.5 us  [radial_filter(): pl.pallas_call(filter_kernel, grid=(rows,), in_specs=[pl.BlockSpec((1, wa...]
    pallas_call x3 -> x4, Pallas kernels: 54 us -> 35.4 us  [radial_transform(): pl.pallas_call(functools.partial(radial_kernel, groups, step), grid_spec=...]
    unnamed x59 -> x49, local copies, waits for them, and re-layouts: 30.7 us -> 23.3 us
    pallas_call x3 -> x4, Pallas kernels: 19.6 us -> 25.1 us  [legendre_transform(): pl.pallas_call(functools.partial(legendre_kernel, groups, spread, parts),...]
    all_to_all x5 -> x6, starting transfers between devices: 28.3 us -> 31.5 us  [move(): return lax.all_to_all(x, BOTH, split_axis=0, concat_axis=0, tiled=True)]
    transpose x10 -> x11, local copies, waits for them, and re-layouts: 16 us -> 13.5 us  [the longest x3 13.3 us: packed(): view[..., lo:hi, :].transpose(3, 4, 1, 5, 2, 0, 6)]
  transfers between devices with their start and end apart: 17 -> 24, of which waited for: 8 -> 17; matrix products, arithmetic and copies ran while one was open for 2% -> 3% of each run, Pallas kernels for 13% -> 16%
where the time goes in v2:
time: 590 us; the launch traced here: 589 us
  waiting for transfers between devices  398 us (67%)
  Pallas kernels  102 us (17%)
  local copies, waits for them, and re-layouts  44.7 us (8%)
  starting transfers between devices  43.3 us (7%)
    ppermute x18, waiting for transfers between devices, exchange(): lax.ppermute(blocks[d], axis, [(i, i ^ d) for i in range(size)])  276 us
    all_to_all x6, waiting for transfers between devices, move(): return lax.all_to_all(x, BOTH, split_axis=0, concat_axis=0, tiled=True)  122 us
    pallas_call x4, Pallas kernels, radial_transform(): pl.pallas_call(functools.partial(radial_kernel, groups, step), grid_spec=...  35.4 us
    all_to_all x6, starting transfers between devices, move(): return lax.all_to_all(x, BOTH, split_axis=0, concat_axis=0, tiled=True)  31.5 us
    pallas_call x4, Pallas kernels, legendre_transform(): pl.pallas_call(functools.partial(legendre_kernel, groups, spread, parts),...  25.1 us
    unnamed x49, local copies, waits for them, and re-layouts  23.3 us
    pallas_call x1, Pallas kernels, radial_filter(): pl.pallas_call(filter_kernel, grid=(rows,), in_specs=[pl.BlockSpec((1, wa...  22.5 us
    pallas_call x4, Pallas kernels, put_in_order(): pl.pallas_call(functools.partial(order_kernel, len(pieces), step), grid_s...  18.7 us
  transfers between devices with their start and end apart: 24, of which 17 were waited for; matrix products, arithmetic and copies ran while one was open for 3% of the time, Pallas kernels for 16%

profile of v2, /device:TPU:0, one launch (start us, length us, event | category | flops | bytes accessed | tf_op | source)
XLA Modules:
  0.0 588.8 jit_solution(18177519033460240874)
XLA Ops:
  0.0 11.9 %copy.34 = bf16[64,2,192,256]{3,0,2,1:T(8,128)(2,1)S(1)} copy(bf16[64,2,192,256]{3,2,1,0:T(8,128)(2,1)} %param.7) | data formatting | bytes 25165824 | tf_op args[0]
  18.7 7.4 %all-to-all-start = ((bf16[32,3,128,256]{3,2,1,0:T(8,128)(2,1)}), bf16[32,3,128,256]{3,2,1,0:T(8,128)(2,1)}, u32[]{:S(2)}, u32[]{:S(2)}) async-start(bf16[32,3,128,256]{3,2,1,0:T(8,128)(2,1)} %bitcast.57), calls=%async_computation | async-start | bytes 12582912 | tf_op jit(solution)/shard_map/all_to_all | solution.py:209
  35.9 6.6 %copy.44 = bf16[8,4,1,3,2,64,256]{6,5,4,3,1,0,2:T(8,128)(2,1)} copy(bf16[8,4,1,3,2,64,256]{6,5,3,1,0,4,2:T(8,128)(2,1)} %get-tuple-element.81) | data formatting | bytes 12582912 | tf_op jit(solution)/shard_map/transpose | solution.py:206
  42.7 22.5 %radial_filter.1.response = bf16[24,512,512]{2,1,0:T(8,128)(2,1)} custom-call(bf16[24,512,512]{2,1,0:T(8,128)(2,1)} %bessel.1, f32[24,1,512]{2,1,0:T(1,128)S(1)} %broadcast_in_dim.32.signal, f32[24,1,512]{2,1,0:T(1,128)S(1)} %broadcast_in_dim.33.noise), custom_call_target="tpu_custom_call" | custom-call | flops 6442450944 | bytes 25165824 | tf_op jit(solution)/shard_map/radial_filter/pallas_call | solution.py:78
  65.3 46.2 %collective-permute-done.1.refs_1_ = bf16[3,768,256]{2,1,0:T(8,128)(2,1)S(1)} collective-permute-done((bf16[3,768,256]{2,1,0:T(8,128)(2,1)}, bf16[3,768,256]{2,1,0:T(8,128)(2,1)S(1)}, u32[]{:S(2)}, u32[]{:S(2)}) %collective-permute-start.1) | collective-permute-done | bytes 1179680 | tf_op jit(solution)/shard_map/ppermute | solution.py:19
  111.5 27.9 %collective-permute-done.2.refs_2_ = bf16[3,768,256]{2,1,0:T(8,128)(2,1)} collective-permute-done((bf16[3,768,256]{2,1,0:T(8,128)(2,1)}, bf16[3,768,256]{2,1,0:T(8,128)(2,1)}, u32[]{:S(2)}, u32[]{:S(2)}) %collective-permute-start.2) | collective-permute-done | bytes 1179680 | tf_op jit(solution)/shard_map/ppermute | solution.py:19
  139.4 26.8 %all-to-all-done = bf16[32,3,128,256]{3,2,1,0:T(8,128)(2,1)} async-done(((bf16[32,3,128,256]{3,2,1,0:T(8,128)(2,1)}), bf16[32,3,128,256]{3,2,1,0:T(8,128)(2,1)}, u32[]{:S(2)}, u32[]{:S(2)}) %all-to-all-start) | async-done | bytes 6291488 | tf_op jit(solution)/shard_map/all_to_all | solution.py:209
  179.2 7.2 %legendre.5 = bf16[768,2048]{1,0:T(8,128)(2,1)} custom-call(s32[25]{0:T(128)S(1)} %pad_add_fusion.1.me.at, bf16[24,768,256]{2,1,0:T(8,128)(2,1)} %own.7, bf16[3,768,256]{2,1,0:T(8,128)(2,1)S(1)} %collective-permute-done.refs_0_, bf16[3,768,256]{2,1,0:T(8,128)(2,1)S(1)} %collective-permute-done.1.refs_1_, ...), custom_call_target="tpu_custom_call" | custom-call | flops 3221225472 | bytes 10485760 | tf_op jit(solution)/shard_map/legendre/pallas_call | solution.py:57
  187.5 69.8 %collective-permute-done.4.refs_1_ = bf16[3,768,256]{2,1,0:T(8,128)(2,1)S(1)} collective-permute-done((bf16[3,768,256]{2,1,0:T(8,128)(2,1)}, bf16[3,768,256]{2,1,0:T(8,128)(2,1)S(1)}, u32[]{:S(2)}, u32[]{:S(2)}) %collective-permute-start.4) | collective-permute-done | bytes 1179680 | tf_op jit(solution)/shard_map/ppermute | solution.py:19
  258.3 26.7 %collective-permute-done.5.refs_2_ = bf16[3,768,256]{2,1,0:T(8,128)(2,1)S(1)} collective-permute-done((bf16[3,768,256]{2,1,0:T(8,128)(2,1)}, bf16[3,768,256]{2,1,0:T(8,128)(2,1)S(1)}, u32[]{:S(2)}, u32[]{:S(2)}) %collective-permute-start.5) | collective-permute-done | bytes 1179680 | tf_op jit(solution)/shard_map/ppermute | solution.py:19
  286.0 25.9 %all-to-all-done.1 = bf16[32,3,128,256]{3,2,1,0:T(8,128)(2,1)} async-done(((bf16[32,3,128,256]{3,2,1,0:T(8,128)(2,1)}), bf16[32,3,128,256]{3,2,1,0:T(8,128)(2,1)}, u32[]{:S(2)}, u32[]{:S(2)}) %all-to-all-start.1) | async-done | bytes 6291488 | tf_op jit(solution)/shard_map/all_to_all | solution.py:209
  325.3 7.2 %legendre.6 = bf16[768,2048]{1,0:T(8,128)(2,1)} custom-call(s32[25]{0:T(128)S(1)} %pad_add_fusion.1.me.at, bf16[24,768,256]{2,1,0:T(8,128)(2,1)} %own.7, bf16[3,768,256]{2,1,0:T(8,128)(2,1)S(1)} %copy-done.1, bf16[3,768,256]{2,1,0:T(8,128)(2,1)S(1)} %copy-done.3, bf16[3,768,256]{2,1,0:T(8,128)(2,1)S(1)} %copy-done.5, ...), custom_call_target="tpu_custom_call" | custom-call | flops 3221225472 | bytes 10485760 | tf_op jit(solution)/shard_map/legendre/pallas_call | solution.py:57
  332.4 22.5 %all-to-all-done.2.coeffs = bf16[32,24,1024]{2,1,0:T(8,128)(2,1)S(1)} async-done(((bf16[32,24,1024]{2,1,0:T(8,128)(2,1)}), bf16[32,24,1024]{2,1,0:T(8,128)(2,1)S(1)}, u32[]{:S(2)}, u32[]{:S(2)}) %all-to-all-start.2) | async-done | bytes 1572896 | tf_op jit(solution)/shard_map/all_to_all | solution.py:209
  359.0 7.3 %radial.4 = (bf16[24,64,128]{2,1,0:T(8,128)(2,1)S(1)}, bf16[24,64,128]{2,1,0:T(8,128)(2,1)S(1)}, bf16[24,64,128]{2,1,0:T(8,128)(2,1)S(1)}, bf16[24,64,128]{2,1,0:T(8,128)(2,1)S(1)}) custom-call(s32[25]{0:T(128)S(1)} %pad_add_fusion.1.me.at, bf16[32,24,1024]{2,1,0:T(8,128)(2,1)S(1)} %all-to-all-done.2.coeffs, s32[64,1]{1,0:T(8,128)S(1)} %copy.45.orders, ...), custom_call_target="tpu_custom_call" | custom-call | flops 805306368 | bytes 15728640 | tf_op jit(solution)/shard_map/radial/pallas_call | solution.py:129
  369.2 28.7 %collective-permute-done.6.refs_0_ = bf16[24,64,128]{2,1,0:T(8,128)(2,1)S(1)} collective-permute-done((bf16[24,64,128]{2,1,0:T(8,128)(2,1)S(1)}, bf16[24,64,128]{2,1,0:T(8,128)(2,1)S(1)}, u32[]{:S(2)}, u32[]{:S(2)}) %collective-permute-start.6) | collective-permute-done | bytes 393248 | tf_op jit(solution)/shard_map/ppermute | solution.py:19
  399.4 7.9 %collective-permute-done.9.refs_0_ = bf16[24,64,128]{2,1,0:T(8,128)(2,1)S(1)} collective-permute-done((bf16[24,64,128]{2,1,0:T(8,128)(2,1)S(1)}, bf16[24,64,128]{2,1,0:T(8,128)(2,1)S(1)}, u32[]{:S(2)}, u32[]{:S(2)}) %collective-permute-start.9) | collective-permute-done | bytes 393248 | tf_op jit(solution)/shard_map/ppermute | solution.py:19
  408.1 22.4 %all-to-all-done.3.coeffs = bf16[32,24,2048]{2,1,0:T(8,128)(2,1)} async-done(((bf16[32,24,2048]{2,1,0:T(8,128)(2,1)}), bf16[32,24,2048]{2,1,0:T(8,128)(2,1)}, u32[]{:S(2)}, u32[]{:S(2)}) %all-to-all-start.3) | async-done | bytes 3145760 | tf_op jit(solution)/shard_map/all_to_all | solution.py:209
  435.2 9.9 %radial.5 = (bf16[24,128,128]{2,1,0:T(8,128)(2,1)S(1)}, bf16[24,128,128]{2,1,0:T(8,128)(2,1)S(1)}, bf16[24,128,128]{2,1,0:T(8,128)(2,1)S(1)}, bf16[24,128,128]{2,1,0:T(8,128)(2,1)S(1)}) custom-call(s32[25]{0:T(128)S(1)} %pad_add_fusion.1.me.at, bf16[32,24,2048]{2,1,0:T(8,128)(2,1)} %all-to-all-done.3.coeffs, s32[128,1]{1,0:T(8,128)S(1)} %copy.46.orders, ...), custom_call_target="tpu_custom_call" | custom-call | flops 1610612736 | bytes 18874368 | tf_op jit(solution)/shard_map/radial/pallas_call | solution.py:129
  449.2 34.6 %collective-permute-done.12.refs_1_ = bf16[24,128,128]{2,1,0:T(8,128)(2,1)S(1)} collective-permute-done((bf16[24,128,128]{2,1,0:T(8,128)(2,1)S(1)}, bf16[24,128,128]{2,1,0:T(8,128)(2,1)S(1)}, u32[]{:S(2)}, u32[]{:S(2)}) %collective-permute-start.12) | collective-permute-done | bytes 786464 | tf_op jit(solution)/shard_map/ppermute | solution.py:19
  483.7 22.1 %collective-permute-done.7.refs_1_ = bf16[24,128,128]{2,1,0:T(8,128)(2,1)S(1)} collective-permute-done((bf16[24,128,128]{2,1,0:T(8,128)(2,1)S(1)}, bf16[24,128,128]{2,1,0:T(8,128)(2,1)S(1)}, u32[]{:S(2)}, u32[]{:S(2)}) %collective-permute-start.7) | collective-permute-done | bytes 786464 | tf_op jit(solution)/shard_map/ppermute | solution.py:19
  511.5 10.9 %radial.6 = (bf16[24,128,128]{2,1,0:T(8,128)(2,1)S(1)}, bf16[24,128,128]{2,1,0:T(8,128)(2,1)}, bf16[24,128,128]{2,1,0:T(8,128)(2,1)}, bf16[24,128,128]{2,1,0:T(8,128)(2,1)}) custom-call(s32[25]{0:T(128)S(1)} %pad_add_fusion.1.me.at, bf16[32,24,2048]{2,1,0:T(8,128)(2,1)} %all-to-all-done.4.coeffs, s32[128,1]{1,0:T(8,128)S(1)} %copy.47.orders, ...), custom_call_target="tpu_custom_call" | custom-call | flops 1610612736 | bytes 18874368 | tf_op jit(solution)/shard_map/radial/pallas_call | solution.py:129
  525.3 23.6 %all-to-all-done.5.coeffs = bf16[32,24,1024]{2,1,0:T(8,128)(2,1)S(1)} async-done(((bf16[32,24,1024]{2,1,0:T(8,128)(2,1)}), bf16[32,24,1024]{2,1,0:T(8,128)(2,1)S(1)}, u32[]{:S(2)}, u32[]{:S(2)}) %all-to-all-start.5) | async-done | bytes 1572896 | tf_op jit(solution)/shard_map/all_to_all | solution.py:209
  548.9 7.3 %radial.7 = (bf16[24,64,128]{2,1,0:T(8,128)(2,1)S(1)}, bf16[24,64,128]{2,1,0:T(8,128)(2,1)S(1)}, bf16[24,64,128]{2,1,0:T(8,128)(2,1)S(1)}, bf16[24,64,128]{2,1,0:T(8,128)(2,1)S(1)}) custom-call(s32[25]{0:T(128)S(1)} %pad_add_fusion.1.me.at, bf16[32,24,1024]{2,1,0:T(8,128)(2,1)S(1)} %all-to-all-done.5.coeffs, s32[64,1]{1,0:T(8,128)S(1)} %copy.48.orders, ...), custom_call_target="tpu_custom_call" | custom-call | flops 805306368 | bytes 15728640 | tf_op jit(solution)/shard_map/radial/pallas_call | solution.py:129
  566.9 9.5 %collective-permute-done.15.refs_3_ = bf16[24,64,128]{2,1,0:T(8,128)(2,1)S(1)} collective-permute-done((bf16[24,64,128]{2,1,0:T(8,128)(2,1)S(1)}, bf16[24,64,128]{2,1,0:T(8,128)(2,1)S(1)}, u32[]{:S(2)}, u32[]{:S(2)}) %collective-permute-start.15) | collective-permute-done | bytes 393248 | tf_op jit(solution)/shard_map/ppermute | solution.py:19
  (123 shorter events, 95.6 us)
Async XLA Ops:
  18.7 147.6 %all-to-all-start = ((bf16[32,3,128,256]{3,2,1,0:T(8,128)(2,1)}), bf16[32,3,128,256]{3,2,1,0:T(8,128)(2,1)}, u32[]{:S(2)}, u32[]{:S(2)}) async-start(bf16[32,3,128,256]{3,2,1,0:T(8,128)(2,1)} %bitcast.57), calls=%async_computation | async-start | bytes 12582912 | tf_op jit(solution)/shard_map/all_to_all | solution.py:209
  32.1 33.2 %collective-permute-start = (bf16[3,768,256]{2,1,0:T(8,128)(2,1)}, bf16[3,768,256]{2,1,0:T(8,128)(2,1)S(1)}, u32[]{:S(2)}, u32[]{:S(2)}) collective-permute-start(bf16[3,768,256]{2,1,0:T(8,128)(2,1)} %get-tuple-element.43), channel_id=1, source_target_pairs={{0,1},{1,0},{2,3},{3,2},{4,5},{5,4},{6,7},{7,6},{8,9},{9,8},{10,11... | collective-permute-start | bytes 3538952 | tf_op jit(solution)/shard_map/ppermute | solution.py:19
  32.3 79.2 %collective-permute-start.1 = (bf16[3,768,256]{2,1,0:T(8,128)(2,1)}, bf16[3,768,256]{2,1,0:T(8,128)(2,1)S(1)}, u32[]{:S(2)}, u32[]{:S(2)}) collective-permute-start(bf16[3,768,256]{2,1,0:T(8,128)(2,1)} %get-tuple-element.44), channel_id=1, source_target_pairs={{0,2},{1,3},{2,0},{3,1},{4,6},{5,7},{6,4},{7,5},{8,10},{9,11},{10,... | collective-permute-start | bytes 3538952 | tf_op jit(solution)/shard_map/ppermute | solution.py:19
  34.0 105.4 %collective-permute-start.2 = (bf16[3,768,256]{2,1,0:T(8,128)(2,1)}, bf16[3,768,256]{2,1,0:T(8,128)(2,1)}, u32[]{:S(2)}, u32[]{:S(2)}) collective-permute-start(bf16[3,768,256]{2,1,0:T(8,128)(2,1)} %get-tuple-element.45), channel_id=1, source_target_pairs={{0,3},{1,2},{2,1},{3,0},{4,7},{5,6},{6,5},{7,4},{8,11},{9,10},{10,... | collective-permute-start | bytes 3538952 | tf_op jit(solution)/shard_map/ppermute | solution.py:19
  166.2 145.7 %all-to-all-start.1 = ((bf16[32,3,128,256]{3,2,1,0:T(8,128)(2,1)}), bf16[32,3,128,256]{3,2,1,0:T(8,128)(2,1)}, u32[]{:S(2)}, u32[]{:S(2)}) async-start(bf16[32,3,128,256]{3,2,1,0:T(8,128)(2,1)} %bitcast.58), calls=%async_computation.1 | async-start | bytes 12582912 | tf_op jit(solution)/shard_map/all_to_all | solution.py:209
  171.8 14.6 %collective-permute-start.3 = (bf16[3,768,256]{2,1,0:T(8,128)(2,1)}, bf16[3,768,256]{2,1,0:T(8,128)(2,1)S(1)}, u32[]{:S(2)}, u32[]{:S(2)}) collective-permute-start(bf16[3,768,256]{2,1,0:T(8,128)(2,1)} %get-tuple-element.51), channel_id=1, source_target_pairs={{0,1},{1,0},{2,3},{3,2},{4,5},{5,4},{6,7},{7,6},{8,9},{9,8},{10,11... | collective-permute-start | bytes 3538952 | tf_op jit(solution)/shard_map/ppermute | solution.py:19
  172.1 85.2 %collective-permute-start.4 = (bf16[3,768,256]{2,1,0:T(8,128)(2,1)}, bf16[3,768,256]{2,1,0:T(8,128)(2,1)S(1)}, u32[]{:S(2)}, u32[]{:S(2)}) collective-permute-start(bf16[3,768,256]{2,1,0:T(8,128)(2,1)} %get-tuple-element.52), channel_id=1, source_target_pairs={{0,2},{1,3},{2,0},{3,1},{4,6},{5,7},{6,4},{7,5},{8,10},{9,11},{10,... | collective-permute-start | bytes 3538952 | tf_op jit(solution)/shard_map/ppermute | solution.py:19
  173.8 111.3 %collective-permute-start.5 = (bf16[3,768,256]{2,1,0:T(8,128)(2,1)}, bf16[3,768,256]{2,1,0:T(8,128)(2,1)S(1)}, u32[]{:S(2)}, u32[]{:S(2)}) collective-permute-start(bf16[3,768,256]{2,1,0:T(8,128)(2,1)} %get-tuple-element.53), channel_id=1, source_target_pairs={{0,3},{1,2},{2,1},{3,0},{4,7},{5,6},{6,5},{7,4},{8,11},{9,10},{10,... | collective-permute-start | bytes 3538952 | tf_op jit(solution)/shard_map/ppermute | solution.py:19
  312.0 43.0 %all-to-all-start.2 = ((bf16[32,24,1024]{2,1,0:T(8,128)(2,1)}), bf16[32,24,1024]{2,1,0:T(8,128)(2,1)S(1)}, u32[]{:S(2)}, u32[]{:S(2)}) async-start(bf16[32,24,1024]{2,1,0:T(8,128)(2,1)} %bitcast.5), calls=%async_computation.2 | async-start | bytes 3145728 | tf_op jit(solution)/shard_map/all_to_all | solution.py:209
  355.0 75.5 %all-to-all-start.3 = ((bf16[32,24,2048]{2,1,0:T(8,128)(2,1)}), bf16[32,24,2048]{2,1,0:T(8,128)(2,1)}, u32[]{:S(2)}, u32[]{:S(2)}) async-start(bf16[32,24,2048]{2,1,0:T(8,128)(2,1)} %bitcast.60), calls=%async_computation.3 | async-start | bytes 6291456 | tf_op jit(solution)/shard_map/all_to_all | solution.py:209
  367.1 30.8 %collective-permute-start.6 = (bf16[24,64,128]{2,1,0:T(8,128)(2,1)S(1)}, bf16[24,64,128]{2,1,0:T(8,128)(2,1)S(1)}, u32[]{:S(2)}, u32[]{:S(2)}) collective-permute-start(bf16[24,64,128]{2,1,0:T(8,128)(2,1)S(1)} %get-tuple-element.57), channel_id=1, source_target_pairs={{0,3},{1,2},{2,1},{3,0},{4,7},{5,6},{6,5},{7,4},{8,11},{9,10},{10,... | collective-permute-start | bytes 1179656 | tf_op jit(solution)/shard_map/ppermute | solution.py:19
  368.4 30.3 %collective-permute-start.8 = (bf16[24,64,128]{2,1,0:T(8,128)(2,1)S(1)}, bf16[24,64,128]{2,1,0:T(8,128)(2,1)S(1)}, u32[]{:S(2)}, u32[]{:S(2)}) collective-permute-start(bf16[24,64,128]{2,1,0:T(8,128)(2,1)S(1)} %get-tuple-element.62), channel_id=1, source_target_pairs={{0,1},{1,0},{2,3},{3,2},{4,5},{5,4},{6,7},{7,6},{8,9},{9,8},{10,11... | collective-permute-start | bytes 1179656 | tf_op jit(solution)/shard_map/ppermute | solution.py:19
  368.8 38.6 %collective-permute-start.9 = (bf16[24,64,128]{2,1,0:T(8,128)(2,1)S(1)}, bf16[24,64,128]{2,1,0:T(8,128)(2,1)S(1)}, u32[]{:S(2)}, u32[]{:S(2)}) collective-permute-start(bf16[24,64,128]{2,1,0:T(8,128)(2,1)S(1)} %get-tuple-element.63), channel_id=1, source_target_pairs={{0,2},{1,3},{2,0},{3,1},{4,6},{5,7},{6,4},{7,5},{8,10},{9,11},{10,... | collective-permute-start | bytes 1179656 | tf_op jit(solution)/shard_map/ppermute | solution.py:19
  430.5 76.4 %all-to-all-start.4 = ((bf16[32,24,2048]{2,1,0:T(8,128)(2,1)}), bf16[32,24,2048]{2,1,0:T(8,128)(2,1)}, u32[]{:S(2)}, u32[]{:S(2)}) async-start(bf16[32,24,2048]{2,1,0:T(8,128)(2,1)} %bitcast.59), calls=%async_computation.4 | async-start | bytes 6291456 | tf_op jit(solution)/shard_map/all_to_all | solution.py:209
  446.0 2.3 collective-permute-start.11
  446.2 37.5 %collective-permute-start.12 = (bf16[24,128,128]{2,1,0:T(8,128)(2,1)S(1)}, bf16[24,128,128]{2,1,0:T(8,128)(2,1)S(1)}, u32[]{:S(2)}, u32[]{:S(2)}) collective-permute-start(bf16[24,128,128]{2,1,0:T(8,128)(2,1)S(1)} %get-tuple-element.72), channel_id=1, source_target_pairs={{0,2},{1,3},{2,0},{3,1},{4,6},{5,7},{6,4},{7,5},{8,10},{9,11},{10,... | collective-permute-start | bytes 2359304 | tf_op jit(solution)/shard_map/ppermute | solution.py:19
  447.9 58.0 %collective-permute-start.7 = (bf16[24,128,128]{2,1,0:T(8,128)(2,1)S(1)}, bf16[24,128,128]{2,1,0:T(8,128)(2,1)S(1)}, u32[]{:S(2)}, u32[]{:S(2)}) collective-permute-start(bf16[24,128,128]{2,1,0:T(8,128)(2,1)S(1)} %get-tuple-element.60), channel_id=1, source_target_pairs={{0,3},{1,2},{2,1},{3,0},{4,7},{5,6},{6,5},{7,4},{8,11},{9,10},{10,... | collective-permute-start | bytes 2359304 | tf_op jit(solution)/shard_map/ppermute | solution.py:19
  506.9 42.0 %all-to-all-start.5 = ((bf16[32,24,1024]{2,1,0:T(8,128)(2,1)}), bf16[32,24,1024]{2,1,0:T(8,128)(2,1)S(1)}, u32[]{:S(2)}, u32[]{:S(2)}) async-start(bf16[32,24,1024]{2,1,0:T(8,128)(2,1)} %bitcast.21), calls=%async_computation.5 | async-start | bytes 3145728 | tf_op jit(solution)/shard_map/all_to_all | solution.py:209
  523.2 34.6 %collective-permute-start.16 = (bf16[24,128,128]{2,1,0:T(8,128)(2,1)}, bf16[24,128,128]{2,1,0:T(8,128)(2,1)}, u32[]{:S(2)}, u32[]{:S(2)}) collective-permute-start(bf16[24,128,128]{2,1,0:T(8,128)(2,1)} %get-tuple-element.68), channel_id=1, source_target_pairs={{0,1},{1,0},{2,3},{3,2},{4,5},{5,4},{6,7},{7,6},{8,9},{9,8},{10,11... | collective-permute-start | bytes 2359304 | tf_op jit(solution)/shard_map/ppermute | solution.py:19
  523.5 43.5 %collective-permute-start.14 = (bf16[24,128,128]{2,1,0:T(8,128)(2,1)}, bf16[24,128,128]{2,1,0:T(8,128)(2,1)}, u32[]{:S(2)}, u32[]{:S(2)}) collective-permute-start(bf16[24,128,128]{2,1,0:T(8,128)(2,1)} %get-tuple-element.69), channel_id=1, source_target_pairs={{0,2},{1,3},{2,0},{3,1},{4,6},{5,7},{6,4},{7,5},{8,10},{9,11},{10,... | collective-permute-start | bytes 2359304 | tf_op jit(solution)/shard_map/ppermute | solution.py:19
  525.2 56.3 %collective-permute-start.10 = (bf16[24,128,128]{2,1,0:T(8,128)(2,1)}, bf16[24,128,128]{2,1,0:T(8,128)(2,1)}, u32[]{:S(2)}, u32[]{:S(2)}) collective-permute-start(bf16[24,128,128]{2,1,0:T(8,128)(2,1)} %get-tuple-element.66), channel_id=1, source_target_pairs={{0,3},{1,2},{2,1},{3,0},{4,7},{5,6},{6,5},{7,4},{8,11},{9,10},{10,... | collective-permute-start | bytes 2359304 | tf_op jit(solution)/shard_map/ppermute | solution.py:19
  556.2 5.7 collective-permute-start.17
  556.3 20.1 %collective-permute-start.15 = (bf16[24,64,128]{2,1,0:T(8,128)(2,1)S(1)}, bf16[24,64,128]{2,1,0:T(8,128)(2,1)S(1)}, u32[]{:S(2)}, u32[]{:S(2)}) collective-permute-start(bf16[24,64,128]{2,1,0:T(8,128)(2,1)S(1)} %get-tuple-element.78), channel_id=1, source_target_pairs={{0,2},{1,3},{2,0},{3,1},{4,6},{5,7},{6,4},{7,5},{8,10},{9,11},{10,... | collective-permute-start | bytes 1179656 | tf_op jit(solution)/shard_map/ppermute | solution.py:19
  557.8 26.0 %collective-permute-start.13 = (bf16[24,64,128]{2,1,0:T(8,128)(2,1)S(1)}, bf16[24,64,128]{2,1,0:T(8,128)(2,1)S(1)}, u32[]{:S(2)}, u32[]{:S(2)}) collective-permute-start(bf16[24,64,128]{2,1,0:T(8,128)(2,1)S(1)} %get-tuple-element.76), channel_id=1, source_target_pairs={{0,3},{1,2},{2,1},{3,0},{4,7},{5,6},{6,5},{7,4},{8,11},{9,10},{10,... | collective-permute-start | bytes 1179656 | tf_op jit(solution)/shard_map/ppermute | solution.py:19
  (24 other events, 172.2 us)

commit v3 on v2

v3 whole, which is shorter than its diff:
```python
import functools
import math

import jax
import jax.numpy as jnp
import numpy as np
from jax import lax
from jax.experimental import pallas as pl
from jax.experimental.pallas import tpu as pltpu
from jax.sharding import Mesh
from jax.sharding import PartitionSpec as P

LANES = 128
HALF = 8
NEAR = ("x", "blk")
SHELL = ("far", "x")
ALL = ("far", "x", "blk")
FIELD_SHARES = (0, 3, 6)
SHARES = (0, 1, 3, 5, 6)
VMEM = 48 * 1024 * 1024


def exchange(blocks, axis, size):
    return [blocks[0]] + [
        lax.ppermute(blocks[d], axis, [(i, i ^ d) for i in range(size)]) for d in range(1, size)
    ]


def legendre_kernel(groups, parts, by_distance, at, own, *refs):
    tables, fields, out = refs[: groups - 1], refs[groups - 1], refs[groups]
    lhs = jnp.concatenate([own[0]] + [t[0] for t in tables], axis=1)
    shells = fields.shape[0]
    height = fields.shape[3] // parts
    near, far, local_rows, _ = out.shape
    width = shells * height
    for c in range(parts):
        rows = [
            jnp.concatenate(
                [fields[s, at[0] ^ d, 0, c * height : (c + 1) * height] for d in range(groups)], axis=1
            )
            for s in range(shells)
        ]
        rhs = jnp.concatenate(rows, axis=0)
        total = lax.dot_general(lhs, rhs, (((1,), (1,)), ((), ())), preferred_element_type=jnp.float32)
        for i in range(far * near):
            device = i % near
            piece = total[i * local_rows : (i + 1) * local_rows].astype(out.dtype)
            out[device ^ at[1] if by_distance else device, i // near, :, c * width : (c + 1) * width] = piece


def legendre_transform(at, own, tables, fields, first, count, per_device, spread, parts, near, by_distance):
    shells, groups, _, height, cycles = fields.shape
    rows = own.shape[1]
    start, offset = first
    width = shells * height
    far = at_far(shells, groups, near)
    local_rows = rows // (near * far)
    grid_spec = pltpu.PrefetchScalarGridSpec(
        num_scalar_prefetch=1,
        grid=(count,),
        in_specs=[
            pl.BlockSpec((1, rows, cycles), lambda u, at: (at[0] // spread * per_device + start + offset + u, 0, 0))
        ]
        + [pl.BlockSpec((1, rows, cycles), lambda u, at: (offset + u, 0, 0))] * (groups - 1)
        + [pl.BlockSpec((shells, groups, 1, height, cycles), lambda u, at: (0, 0, offset + u, 0, 0))],
        out_specs=pl.BlockSpec((near, far, local_rows, width), lambda u, at: (0, 0, 0, u)),
    )
    flops = 2 * count * rows * width * cycles * groups
    return pl.pallas_call(
        functools.partial(legendre_kernel, groups, parts, by_distance),
        grid_spec=grid_spec,
        out_shape=jax.ShapeDtypeStruct((near, far, local_rows, count * width), jnp.bfloat16),
        compiler_params=pltpu.CompilerParams(vmem_limit_bytes=VMEM),
        cost_estimate=pl.CostEstimate(
            flops=flops, bytes_accessed=2 * count * (rows * width + groups * cycles * (rows + width)), transcendentals=0
        ),
        name="legendre",
    )(at, own, *tables, fields)


def at_far(shells, groups, near):
    return shells * groups // near


def regroup_kernel(count, at, *refs):
    ins, outs = refs[:count], refs[count:]
    for e, out in enumerate(outs):
        for d in range(count):
            out[at[1] ^ d] = ins[d][at[2] ^ e]


def regroup(at, blocks):
    near = len(blocks)
    far, rows, columns = blocks[0].shape
    lanes = columns // 2 if columns % (2 * LANES) == 0 else columns
    specs = [pl.BlockSpec((far, rows, lanes), lambda t, at: (0, 0, t))] * near
    return pl.pallas_call(
        functools.partial(regroup_kernel, len(blocks)),
        grid_spec=pltpu.PrefetchScalarGridSpec(
            num_scalar_prefetch=1,
            grid=(columns // lanes,),
            in_specs=specs,
            out_specs=[pl.BlockSpec((near, rows, lanes), lambda t, at: (0, 0, t))] * far,
        ),
        out_shape=[jax.ShapeDtypeStruct((near, rows, columns), jnp.bfloat16)] * far,
        compiler_params=pltpu.CompilerParams(vmem_limit_bytes=VMEM),
        cost_estimate=pl.CostEstimate(flops=0, bytes_accessed=4 * near * far * rows * columns, transcendentals=0),
        name="regroup",
    )(at, *blocks)


def filter_kernel(groups, at, bessel, signal, noise, out, held):
    for t in range(bessel.shape[0]):
        wiener = signal[t] / (signal[t] + noise[t])
        turned = (bessel[t].astype(jnp.float32).T * wiener).astype(jnp.bfloat16)
        response = jnp.dot(turned, bessel[t], preferred_element_type=jnp.float32).astype(out.dtype)
        width = response.shape[0] // groups
        for b in range(groups):
            held[b] = response[b * width : (b + 1) * width]
        for d in range(groups):
            out[t, d * width : (d + 1) * width] = held[at[0] ^ d]


def radial_filter(at, bessel, signal, noise, groups):
    rows, waves, shells = bessel.shape
    return pl.pallas_call(
        functools.partial(filter_kernel, groups),
        grid_spec=pltpu.PrefetchScalarGridSpec(
            num_scalar_prefetch=1,
            grid=(rows,),
            in_specs=[
                pl.BlockSpec((1, waves, shells), lambda t, at: (t, 0, 0)),
                pl.BlockSpec((1, 1, waves), lambda t, at: (t, 0, 0)),
                pl.BlockSpec((1, 1, waves), lambda t, at: (t, 0, 0)),
            ],
            out_specs=pl.BlockSpec((1, shells, shells), lambda t, at: (t, 0, 0)),
            scratch_shapes=[pltpu.VMEM((groups, shells // groups, shells), jnp.bfloat16)],
        ),
        out_shape=jax.ShapeDtypeStruct((rows, shells, shells), jnp.bfloat16),
        compiler_params=pltpu.CompilerParams(vmem_limit_bytes=VMEM),
        cost_estimate=pl.CostEstimate(
            flops=2 * rows * waves * shells * shells, bytes_accessed=4 * rows * shells * waves, transcendentals=0
        ),
        name="radial_filter",
    )(at, bessel, signal, noise)


def radial_kernel(groups, far, step, slices, at, *refs):
    ins, orders, responses = refs[:far], refs[far], refs[far + 1 : far + 1 + slices]
    outs, coeffs = refs[far + 1 + slices : -1], refs[-1]
    near = ins[0].shape[0]
    if far == 1:
        coeffs = ins[0]
    else:
        for e in range(far):
            coeffs[pl.ds((at[2] ^ e) * near, near)] = ins[e][...]
    first = pl.program_id(0) * step
    length = responses[0].shape[1]
    width = length // groups
    columns = orders.shape[0]
    fold = outs[0].shape[2] // columns
    senders = near * far
    pieces = coeffs.shape[2] // length
    if step % HALF == 0:
        size = senders * step
        to = lax.broadcasted_iota(jnp.int32, (size, size), 0)
        source = lax.broadcasted_iota(jnp.int32, (size, size), 1)
        pick = jnp.where(source == to % senders * step + to // senders, 1.0, 0.0).astype(coeffs.dtype)
        flat = coeffs[...].reshape(size, coeffs.shape[2])
        turned = jnp.dot(pick, flat, preferred_element_type=jnp.float32).astype(coeffs.dtype)
        rows = [turned[t * senders : (t + 1) * senders] for t in range(step)]
    else:
        rows = [coeffs[:, t, :] for t in range(step)]
    for t in range(step):
        row = jnp.concatenate([rows[t][:, n * length : (n + 1) * length] for n in range(pieces)], axis=0)
        allowed = at[3 + first + t] >= orders[...]
        masked = jnp.where(allowed, row, jnp.zeros((), row.dtype))
        response = responses[t * slices // step][t % (step // slices)]
        back = lax.dot_general(response, masked, (((1,), (1,)), ((), ())), preferred_element_type=jnp.float32)
        back = back.astype(coeffs.dtype)
        part = width // fold
        for d in range(groups):
            parts = [back[d * width + h * part : d * width + (h + 1) * part] for h in range(fold)]
            outs[d][t] = parts[0] if fold == 1 else jnp.concatenate(parts, axis=1)


def folding(columns):
    return LANES // columns if columns < LANES and LANES % columns == 0 else 1


def radial_transform(at, blocks, orders, response, groups):
    near, rows, lanes = blocks[0].shape
    far = len(blocks)
    length = response.shape[1]
    columns = orders.shape[0]
    fold = folding(columns)
    shape = (length // groups // fold, columns * fold)
    step = 8 if rows % 8 == 0 else rows
    slices = math.gcd(step, 4)
    grid_spec = pltpu.PrefetchScalarGridSpec(
        num_scalar_prefetch=1,
        grid=(rows // step,),
        in_specs=[pl.BlockSpec((near, step, lanes), lambda t, at: (0, t, 0))] * far
        + [
            pl.BlockSpec((columns, 1), lambda t, at: (0, 0)),
        ]
        + [
            pl.BlockSpec((step // slices, length, length), lambda t, at, q=q: (t * slices + q, 0, 0))
            for q in range(slices)
        ],
        out_specs=[pl.BlockSpec((step, *shape), lambda t, at: (t, 0, 0))] * groups,
        scratch_shapes=[
            pltpu.VMEM((far * near if far > 1 else 1, step, lanes), jnp.bfloat16),
        ],
    )
    return pl.pallas_call(
        functools.partial(radial_kernel, groups, far, step, slices),
        grid_spec=grid_spec,
        out_shape=[jax.ShapeDtypeStruct((rows, *shape), jnp.bfloat16)] * groups,
        compiler_params=pltpu.CompilerParams(vmem_limit_bytes=VMEM),
        cost_estimate=pl.CostEstimate(
            flops=2 * rows * columns * length * length,
            bytes_accessed=2 * rows * (length * length + 2 * columns * length),
            transcendentals=0,
        ),
        name="radial",
    )(at, *blocks, orders, *[response] * slices)


def order_kernel(pieces, step, me, *refs):
    ins, place, out = refs[:pieces], refs[pieces], refs[-1]
    runs = place.shape[0]
    part = out.shape[1] // runs
    for h in range(runs):
        rows = []
        for t in range(step):
            rows.append(
                jnp.concatenate([p[t] if p.shape[1] == part else p[t, h * part : (h + 1) * part] for p in ins], axis=1)
            )
        mixed = jnp.dot(jnp.concatenate(rows, axis=0), place[h], preferred_element_type=jnp.float32)
        for t in range(step):
            out[t, h * part : (h + 1) * part] = mixed[t * part : (t + 1) * part].astype(out.dtype)


def placement(columns_of, total):
    runs = max(folding(columns.size) for columns in columns_of)
    matrices = []
    for h in range(runs):
        blocks = []
        for columns in columns_of:
            fold = folding(columns.size)
            block = (columns[:, None] == np.arange(total)[None, :]).astype(np.float32)
            blocks += [block if fold == 1 or k == h else 0 * block for k in range(fold)]
        matrices.append(np.concatenate(blocks))
    return jnp.asarray(np.stack(matrices), jnp.bfloat16)


def put_in_order(me, pieces, place, distance, so_far, groups, width):
    rows = pieces[0].shape[0]
    columns = place.shape[2]
    step = 8 if rows % 8 == 0 else rows
    specs = [pl.BlockSpec((step, *p.shape[1:]), lambda t, me: (t, 0, 0)) for p in pieces]
    specs.append(pl.BlockSpec(place.shape, lambda t, me: (0, 0, 0)))
    operands = list(pieces) + [place]
    aliases = {}
    if so_far is not None:
        specs.append(pl.BlockSpec(memory_space=pl.ANY))
        operands.append(so_far)
        aliases = {len(operands): 0}
    grid_spec = pltpu.PrefetchScalarGridSpec(
        num_scalar_prefetch=1,
        grid=(rows // step,),
        in_specs=specs,
        out_specs=pl.BlockSpec((step, width, columns), lambda t, me: ((me[0] ^ distance) * (rows // step) + t, 0, 0)),
    )
    return pl.pallas_call(
        functools.partial(order_kernel, len(pieces), step),
        grid_spec=grid_spec,
        out_shape=jax.ShapeDtypeStruct((groups * rows, width, columns), jnp.bfloat16),
        input_output_aliases=aliases,
        compiler_params=pltpu.CompilerParams(vmem_limit_bytes=VMEM),
        cost_estimate=pl.CostEstimate(
            flops=2 * rows * width * columns * place.shape[1], bytes_accessed=4 * rows * width * columns, transcendentals=0
        ),
        name="in_order",
    )(me, *operands)


def pack_kernel(*refs):
    xs, pick, out = refs[:-2], refs[-2], refs[-1]
    here = xs[0].shape[0] * len(xs)
    shell_blocks, sharers, _, columns = out.shape[:4]
    depth = xs[0].shape[2] * HALF
    for g in range(0, here, 2 * HALF):
        x, start = xs[g * len(xs) // here], g % (here // len(xs))
        found = [
            jnp.dot(
                pick[...],
                x[start + h : start + h + HALF, 0].reshape(depth, x.shape[3]),
                preferred_element_type=jnp.float32,
            )
            for h in (0, HALF)
        ]
        for n in range(shell_blocks * sharers * columns):
            rows = jnp.concatenate([f[n * HALF : (n + 1) * HALF] for f in found], axis=0)
            block, rest = divmod(n, sharers * columns)
            out[block, rest // columns, 0, rest % columns, 0, g : g + 2 * HALF] = rows.astype(out.dtype)


def pack(x, span, shells, sharers, spread):
    here, complex_parts, orders, cycles = x.shape
    lo, hi = span
    columns, parts = hi - lo, complex_parts // spread
    local = orders // shells
    per_device = local // sharers
    together = 2 * HALF // math.gcd(local, 2 * HALF)
    block, sharer, column, row = np.ix_(range(together), range(sharers), range(lo, hi), range(HALF))
    source = (row * together * local + block * local + sharer * per_device + column).reshape(-1, 1)
    pick = jnp.asarray(source == np.arange(HALF * together * local), jnp.bfloat16)
    shape = (shells, sharers, spread, columns, parts, here, cycles)
    slices = math.gcd(here // (2 * HALF), 4)
    return pl.pallas_call(
        pack_kernel,
        grid=(shells // together, complex_parts),
        in_specs=[
            *[
                pl.BlockSpec((here // slices, 1, together * local, cycles), lambda b, c, q=q: (q, c, b, 0))
                for q in range(slices)
            ],
            pl.BlockSpec(pick.shape, lambda b, c: (0, 0)),
        ],
        out_specs=pl.BlockSpec(
            (together, sharers, 1, columns, 1, here, cycles), lambda b, c: (b, 0, c // parts, 0, c % parts, 0, 0)
        ),
        out_shape=jax.ShapeDtypeStruct(shape, jnp.bfloat16),
        compiler_params=pltpu.CompilerParams(vmem_limit_bytes=VMEM),
        cost_estimate=pl.CostEstimate(
            flops=2 * pick.size * cycles * here // HALF * complex_parts * shells // together,
            bytes_accessed=2 * x.size + 2 * math.prod(shape),
            transcendentals=0,
        ),
        name="pack",
    )(*[x] * slices, pick)


def body(cycle_fourier, legendre, azimuth_orders, multipole, bessel, signal_power, noise_power):
    far, groups = lax.axis_size("far"), lax.axis_size("blk")
    shells = far * lax.axis_size("x")
    devices = shells * groups
    near = devices // far
    here, complex_parts, orders, cycles = cycle_fourier.shape
    local_orders, rows, _ = legendre.shape
    local_rows = multipole.shape[0]
    sharers = math.gcd(local_orders, groups)
    spread = groups // sharers
    per_device = local_orders // sharers
    parts = complex_parts // spread
    me = lax.axis_index("blk").astype(jnp.int32)
    indices = [lax.axis_index(name).astype(jnp.int32).reshape(1) for name in ("blk", NEAR, "far")]
    at = jnp.concatenate(indices + [multipole])

    cuts = [round(per_device * share / FIELD_SHARES[-1]) for share in FIELD_SHARES]
    spans = [(lo, hi) for lo, hi in zip(cuts, cuts[1:]) if hi > lo]
    cuts = [round(per_device * share / SHARES[-1]) for share in SHARES]
    chunks = [(lo, hi) for lo, hi in zip(cuts, cuts[1:]) if hi > lo]

    def packed(span):
        blocks = pack(cycle_fourier, span, shells, sharers, spread)
        return blocks.reshape(devices, span[1] - span[0], parts * here, cycles)

    def move(x, axes):
        return lax.all_to_all(x, axes, split_axis=0, concat_axis=0, tiled=True)

    def send_tables(span, earlier):
        lo, hi = span
        blocks = [
            lax.dynamic_slice_in_dim(legendre, (me ^ d) // spread * per_device + lo, hi - lo, 0) for d in range(1, groups)
        ]
        return exchange([None] + after(earlier, blocks), "blk", groups)[1:]

    def after(earlier, later):
        return lax.optimization_barrier((earlier, later))[1]

    order_view = azimuth_orders.reshape(shells, sharers, 1, per_device, 1)
    column_view = np.arange(orders * complex_parts).reshape(shells, sharers, per_device, spread, parts)
    limits, places = [], []
    for lo, hi in chunks:
        limit = jnp.broadcast_to(order_view[:, :, :, lo:hi], (shells, sharers, spread, hi - lo, parts))
        limits.append(limit.transpose(3, 4, 0, 1, 2).reshape(-1, 1))
        places.append(column_view[:, :, lo:hi].transpose(2, 4, 0, 1, 3).reshape(-1))
    place = placement(places, orders * complex_parts)
    response = radial_filter(at, bessel, signal_power[:, None, :], noise_power[:, None, :], groups)

    def coefficients(k, by_distance=False):
        lo, hi = chunks[k]
        which = max(i for i, span in enumerate(spans) if span[0] <= lo)
        start = spans[which][0]
        source = fields[which].reshape(shells, groups, *fields[which].shape[1:])
        sent = legendre_transform(
            at,
            legendre,
            tables[which],
            source,
            (start, lo - start),
            hi - lo,
            per_device,
            spread,
            parts,
            near if by_distance else devices,
            by_distance,
        )
        return sent if by_distance else sent.reshape(devices, local_rows, -1)

    fields = [move(packed(spans[0]), ALL)]
    tables = [send_tables(spans[0], ())]
    late, _ = lax.optimization_barrier((packed(spans[1]), (fields, tables, response, limits)))
    fields.append(move(late, ALL))
    first = coefficients(0, True)
    blocks = exchange([first[d] for d in range(near)], NEAR, near)
    tables.append(send_tables(spans[1], (fields[0], blocks)))
    arrived = exchange(regroup(at, blocks), "far", far)
    count = len(chunks)
    sent = [coefficients(k) for k in range(1, count)]
    ready = [x for x, chunk in zip(sent, chunks[1:]) if chunk[0] < spans[0][1]]
    before = [arrived, fields, tables, ready]
    outs, gathered = [], []
    for k in range(count):
        if k + 1 < count:
            coming = move(after(before, sent[k]), ALL)
        elif k >= 1:
            arrived = after((outs[k - 1], gathered[: k - 1]), arrived)
        outs.append(radial_transform(at, arrived, limits[k], response, groups))
        gathered.append(exchange(outs[k], "blk", groups))
        arrived = [coming]
        before = [coming, sent, gathered[k]]

    out = None
    for d in range(groups):
        out = put_in_order(at, [g[d] for g in gathered], place, d, out, groups, shells * here // groups)
    return out


def solution(mesh):
    shells, groups = mesh.shape["shell"], mesh.shape["blk"]
    far = 1 << shells.bit_length() // 2
    split = Mesh(mesh.devices.reshape(far, shells // far, groups), ALL)
    rows = P(ALL)
    return jax.shard_map(
        body,
        mesh=split,
        in_specs=(P(SHELL, None, None, "blk"), P(SHELL, None, "blk"), P(), rows, rows, rows, rows),
        out_specs=P(SHELL, "blk", None),
        check_vma=False,
    )
```

time: 590 us -> 580 us (0.983)
  waiting for transfers between devices: 398 us -> 358 us
  Pallas kernels: 102 us -> 125 us
  starting transfers between devices: 43.3 us -> 57.8 us
  local copies, waits for them, and re-layouts: 44.7 us -> 36.9 us
    all_to_all x6 -> x5, waiting for transfers between devices: 122 us -> 72.6 us  [move(): return lax.all_to_all(x, axes, split_axis=0, concat_axis=0, tiled=True)]
    pallas_call x9 -> x12, Pallas kernels: 83 us -> 106 us  [the longest x4 36 us: radial_transform(): pl.pallas_call(functools.partial(radial_kernel, groups, far, step, slices...]
    transpose x5 -> x0, local copies, waits for them, and re-layouts: 13.3 us -> none  [the longest x3 13.3 us: packed(): view[..., lo:hi, :].transpose(3, 4, 1, 5, 2, 0, 6)]
    ppermute x18 -> x28, starting transfers between devices: 11.7 us -> 23.5 us  [exchange(): lax.ppermute(blocks[d], axis, [(i, i ^ d) for i in range(size)])]
    unnamed x49 -> x80, local copies, waits for them, and re-layouts: 23.3 us -> 13.1 us
    ppermute x18 -> x28, waiting for transfers between devices: 276 us -> 285 us  [exchange(): lax.ppermute(blocks[d], axis, [(i, i ^ d) for i in range(size)])]
    all_to_all x6 -> x5, starting transfers between devices: 31.5 us -> 34.3 us  [move(): return lax.all_to_all(x, axes, split_axis=0, concat_axis=0, tiled=True)]
  transfers between devices with their start and end apart: 24 -> 33, of which waited for: 17 -> 20; matrix products, arithmetic and copies ran while one was open for 3% -> 4% of each run, Pallas kernels for 16% -> 19%
where the time goes in v3:
time: 580 us; the launch traced here: 578 us
  waiting for transfers between devices  358 us (62%)
  Pallas kernels  125 us (22%)
  starting transfers between devices  57.8 us (10%)
  local copies, waits for them, and re-layouts  36.9 us (6%)
    ppermute x28, waiting for transfers between devices, exchange(): lax.ppermute(blocks[d], axis, [(i, i ^ d) for i in range(size)])  285 us
    all_to_all x5, waiting for transfers between devices, move(): return lax.all_to_all(x, axes, split_axis=0, concat_axis=0, tiled=True)  72.6 us
    pallas_call x4, Pallas kernels, radial_transform(): pl.pallas_call(functools.partial(radial_kernel, groups, far, step, slices...  36 us
    all_to_all x5, starting transfers between devices, move(): return lax.all_to_all(x, axes, split_axis=0, concat_axis=0, tiled=True)  34.3 us
    pallas_call x4, Pallas kernels, legendre_transform(): pl.pallas_call(functools.partial(legendre_kernel, groups, parts, by_dista...  23.6 us
    ppermute x28, starting transfers between devices, exchange(): lax.ppermute(blocks[d], axis, [(i, i ^ d) for i in range(size)])  23.5 us
    pallas_call x1, Pallas kernels, radial_filter(): pl.pallas_call(functools.partial(filter_kernel, groups), grid_spec=pltpu....  23.4 us
    pallas_call x2, Pallas kernels, pack(): pl.pallas_call(pack_kernel, grid=(shells // together, complex_parts), in_...  22 us
  transfers between devices with their start and end apart: 33, of which 20 were waited for; matrix products, arithmetic and copies ran while one was open for 4% of the time, Pallas kernels for 19%

profile of v3, /device:TPU:0, one launch (start us, length us, event | category | flops | bytes accessed | tf_op | source)
XLA Modules:
  0.0 578.2 jit_solution(7101583559347682022)
XLA Ops:
  0.9 10.9 %pack.2 = bf16[8,4,1,3,2,64,256]{6,5,4,3,2,1,0:T(8,128)(2,1)} custom-call(bf16[64,2,192,256]{3,2,1,0:T(8,128)(2,1)} %refs_3_.3, bf16[64,2,192,256]{3,2,1,0:T(8,128)(2,1)} %refs_3_.3, bf16[64,2,192,256]{3,2,1,0:T(8,128)(2,1)} %refs_3_.3, bf16[64,2,192,256]{3,2,1,0:T(8,128)(2,1)} %refs_3_.3, bf16[192,384]{1,0:T(8,128)(2,1)S(1)} %copy-done.31), custom_call_target="tpu_custom_call" | custom-call | flops 2415919104 | bytes 18874368 | tf_op jit(solution)/shard_map/pack/pallas_call | solution.py:322
  44.9 11.1 %pack.3 = bf16[8,4,1,3,2,64,256]{6,5,4,3,2,1,0:T(8,128)(2,1)} custom-call(bf16[64,2,192,256]{3,2,1,0:T(8,128)(2,1)} %refs_3_.3, bf16[64,2,192,256]{3,2,1,0:T(8,128)(2,1)} %refs_3_.3, bf16[64,2,192,256]{3,2,1,0:T(8,128)(2,1)} %refs_3_.3, bf16[64,2,192,256]{3,2,1,0:T(8,128)(2,1)} %refs_3_.3, bf16[192,384]{1,0:T(8,128)(2,1)S(1)} %copy-done.30), custom_call_target="tpu_custom_call" | custom-call | flops 2415919104 | bytes 18874368 | tf_op jit(solution)/shard_map/pack/pallas_call | solution.py:322
  56.0 23.4 %radial_filter.1.refs_5_.refs_6_.refs_7_.refs_8_.refs_2_.refs_3_.refs_4_ = bf16[24,512,512]{2,1,0:T(8,128)(2,1)} custom-call(s32[27]{0:T(128)S(1)} %pad_add_fusion.at.me, bf16[24,512,512]{2,1,0:T(8,128)(2,1)} %bessel.1, f32[24,1,512]{2,1,0:T(1,128)S(1)} %copy-done.28, f32[24,1,512]{2,1,0:T(1,128)S(1)} %copy-done.29), custom_call_target="tpu_custom_call" | custom-call | flops 6442450944 | bytes 25165824 | tf_op jit(solution)/shard_map/radial_filter/pallas_call | solution.py:126
  79.4 25.3 %collective-permute-done.1.refs_1_ = bf16[3,768,256]{2,1,0:T(8,128)(2,1)S(1)} collective-permute-done((bf16[3,768,256]{2,1,0:T(8,128)(2,1)}, bf16[3,768,256]{2,1,0:T(8,128)(2,1)S(1)}, u32[]{:S(2)}, u32[]{:S(2)}) %collective-permute-start.1) | collective-permute-done | bytes 1179680 | tf_op jit(solution)/shard_map/ppermute | solution.py:25
  104.7 27.8 %collective-permute-done.2.refs_2_ = bf16[3,768,256]{2,1,0:T(8,128)(2,1)S(1)} collective-permute-done((bf16[3,768,256]{2,1,0:T(8,128)(2,1)}, bf16[3,768,256]{2,1,0:T(8,128)(2,1)S(1)}, u32[]{:S(2)}, u32[]{:S(2)}) %collective-permute-start.2) | collective-permute-done | bytes 1179680 | tf_op jit(solution)/shard_map/ppermute | solution.py:25
  132.5 26.9 %all-to-all-done = bf16[32,3,128,256]{3,2,1,0:T(8,128)(2,1)} async-done(((bf16[32,3,128,256]{3,2,1,0:T(8,128)(2,1)}), bf16[32,3,128,256]{3,2,1,0:T(8,128)(2,1)}, u32[]{:S(2)}, u32[]{:S(2)}) %all-to-all-start) | async-done | bytes 6291488 | tf_op jit(solution)/shard_map/all_to_all | solution.py:372
  175.7 33.9 %collective-permute-done.4.refs_2_ = bf16[4,24,1024]{2,1,0:T(8,128)(2,1)S(1)} collective-permute-done((bf16[4,24,1024]{2,1,0:T(8,128)(2,1)S(1)}, bf16[4,24,1024]{2,1,0:T(8,128)(2,1)S(1)}, u32[]{:S(2)}, u32[]{:S(2)}) %collective-permute-start.4) | collective-permute-done | bytes 196640 | tf_op jit(solution)/shard_map/ppermute | solution.py:25
  213.3 8.7 %collective-permute-done.6.refs_4_ = bf16[4,24,1024]{2,1,0:T(8,128)(2,1)S(1)} collective-permute-done((bf16[4,24,1024]{2,1,0:T(8,128)(2,1)S(1)}, bf16[4,24,1024]{2,1,0:T(8,128)(2,1)S(1)}, u32[]{:S(2)}, u32[]{:S(2)}) %collective-permute-start.6) | collective-permute-done | bytes 196640 | tf_op jit(solution)/shard_map/ppermute | solution.py:25
  222.0 7.9 %collective-permute-done.7.refs_5_ = bf16[4,24,1024]{2,1,0:T(8,128)(2,1)S(1)} collective-permute-done((bf16[4,24,1024]{2,1,0:T(8,128)(2,1)S(1)}, bf16[4,24,1024]{2,1,0:T(8,128)(2,1)S(1)}, u32[]{:S(2)}, u32[]{:S(2)}) %collective-permute-start.7) | collective-permute-done | bytes 196640 | tf_op jit(solution)/shard_map/ppermute | solution.py:25
  229.9 10.3 %collective-permute-done.8.refs_6_ = bf16[4,24,1024]{2,1,0:T(8,128)(2,1)S(1)} collective-permute-done((bf16[4,24,1024]{2,1,0:T(8,128)(2,1)S(1)}, bf16[4,24,1024]{2,1,0:T(8,128)(2,1)S(1)}, u32[]{:S(2)}, u32[]{:S(2)}) %collective-permute-start.8) | collective-permute-done | bytes 196640 | tf_op jit(solution)/shard_map/ppermute | solution.py:25
  247.7 29.5 %collective-permute-done.10.refs_1_ = bf16[8,24,1024]{2,1,0:T(8,128)(2,1)S(1)} collective-permute-done((bf16[8,24,1024]{2,1,0:T(8,128)(2,1)S(1)}, bf16[8,24,1024]{2,1,0:T(8,128)(2,1)S(1)}, u32[]{:S(2)}, u32[]{:S(2)}) %collective-permute-start.10) | collective-permute-done | bytes 393248 | tf_op jit(solution)/shard_map/ppermute | solution.py:25
  287.7 43.2 %collective-permute-done.11.refs_2_ = bf16[8,24,1024]{2,1,0:T(8,128)(2,1)S(1)} collective-permute-done((bf16[8,24,1024]{2,1,0:T(8,128)(2,1)S(1)}, bf16[8,24,1024]{2,1,0:T(8,128)(2,1)S(1)}, u32[]{:S(2)}, u32[]{:S(2)}) %collective-permute-start.11) | collective-permute-done | bytes 393248 | tf_op jit(solution)/shard_map/ppermute | solution.py:25
  335.5 12.0 %all-to-all-start.2 = ((bf16[32,24,2048]{2,1,0:T(8,128)(2,1)}), bf16[32,24,2048]{2,1,0:T(8,128)(2,1)}, u32[]{:S(2)}, u32[]{:S(2)}) async-start(bf16[32,24,2048]{2,1,0:T(8,128)(2,1)} %bitcast.46), calls=%async_computation.2 | async-start | bytes 6291456 | tf_op jit(solution)/shard_map/all_to_all | solution.py:372
  347.7 8.7 %radial.4 = (bf16[24,64,128]{2,1,0:T(8,128)(2,1)S(1)}, bf16[24,64,128]{2,1,0:T(8,128)(2,1)S(1)}, bf16[24,64,128]{2,1,0:T(8,128)(2,1)S(1)}, bf16[24,64,128]{2,1,0:T(8,128)(2,1)S(1)}) custom-call(s32[27]{0:T(128)S(1)} %pad_add_fusion.at.me, bf16[8,24,1024]{2,1,0:T(8,128)(2,1)S(1)} %copy-done.14, bf16[8,24,1024]{2,1,0:T(8,128)(2,1)S(1)} %copy-done.16, ...), custom_call_target="tpu_custom_call" | custom-call | flops 805306368 | bytes 15728640 | tf_op jit(solution)/shard_map/radial/pallas_call | solution.py:216
  371.0 15.7 %collective-permute-done.13.refs_0_ = bf16[24,64,128]{2,1,0:T(8,128)(2,1)S(1)} collective-permute-done((bf16[24,64,128]{2,1,0:T(8,128)(2,1)S(1)}, bf16[24,64,128]{2,1,0:T(8,128)(2,1)S(1)}, u32[]{:S(2)}, u32[]{:S(2)}) %collective-permute-start.13) | collective-permute-done | bytes 393248 | tf_op jit(solution)/shard_map/ppermute | solution.py:25
  388.2 7.9 %collective-permute-done.19.refs_0_ = bf16[24,64,128]{2,1,0:T(8,128)(2,1)S(1)} collective-permute-done((bf16[24,64,128]{2,1,0:T(8,128)(2,1)S(1)}, bf16[24,64,128]{2,1,0:T(8,128)(2,1)S(1)}, u32[]{:S(2)}, u32[]{:S(2)}) %collective-permute-start.19) | collective-permute-done | bytes 393248 | tf_op jit(solution)/shard_map/ppermute | solution.py:25
  396.9 22.4 %all-to-all-done.2.refs_0_ = bf16[32,24,2048]{2,1,0:T(8,128)(2,1)} async-done(((bf16[32,24,2048]{2,1,0:T(8,128)(2,1)}), bf16[32,24,2048]{2,1,0:T(8,128)(2,1)}, u32[]{:S(2)}, u32[]{:S(2)}) %all-to-all-start.2) | async-done | bytes 3145760 | tf_op jit(solution)/shard_map/all_to_all | solution.py:372
  424.2 8.9 %radial.5 = (bf16[24,128,128]{2,1,0:T(8,128)(2,1)S(1)}, bf16[24,128,128]{2,1,0:T(8,128)(2,1)S(1)}, bf16[24,128,128]{2,1,0:T(8,128)(2,1)S(1)}, bf16[24,128,128]{2,1,0:T(8,128)(2,1)S(1)}) custom-call(s32[27]{0:T(128)S(1)} %pad_add_fusion.at.me, bf16[32,24,2048]{2,1,0:T(8,128)(2,1)} %all-to-all-done.2.refs_0_, s32[128,1]{1,0:T(8,128)S(1)} %copy.31.refs_1_, ...), custom_call_target="tpu_custom_call" | custom-call | flops 1610612736 | bytes 18874368 | tf_op jit(solution)/shard_map/radial/pallas_call | solution.py:216
  436.1 36.4 %collective-permute-done.17.refs_1_ = bf16[24,128,128]{2,1,0:T(8,128)(2,1)S(1)} collective-permute-done((bf16[24,128,128]{2,1,0:T(8,128)(2,1)S(1)}, bf16[24,128,128]{2,1,0:T(8,128)(2,1)S(1)}, u32[]{:S(2)}, u32[]{:S(2)}) %collective-permute-start.17) | collective-permute-done | bytes 786464 | tf_op jit(solution)/shard_map/ppermute | solution.py:25
  473.4 21.2 %collective-permute-done.22.refs_1_ = bf16[24,128,128]{2,1,0:T(8,128)(2,1)S(1)} collective-permute-done((bf16[24,128,128]{2,1,0:T(8,128)(2,1)S(1)}, bf16[24,128,128]{2,1,0:T(8,128)(2,1)S(1)}, u32[]{:S(2)}, u32[]{:S(2)}) %collective-permute-start.22) | collective-permute-done | bytes 786464 | tf_op jit(solution)/shard_map/ppermute | solution.py:25
  501.7 10.2 %radial.6 = (bf16[24,128,128]{2,1,0:T(8,128)(2,1)S(1)}, bf16[24,128,128]{2,1,0:T(8,128)(2,1)}, bf16[24,128,128]{2,1,0:T(8,128)(2,1)}, bf16[24,128,128]{2,1,0:T(8,128)(2,1)}) custom-call(s32[27]{0:T(128)S(1)} %pad_add_fusion.at.me, bf16[32,24,2048]{2,1,0:T(8,128)(2,1)} %all-to-all-done.3.refs_0_, s32[128,1]{1,0:T(8,128)S(1)} %copy-done.27, ...), custom_call_target="tpu_custom_call" | custom-call | flops 1610612736 | bytes 18874368 | tf_op jit(solution)/shard_map/radial/pallas_call | solution.py:216
  515.4 22.2 %all-to-all-done.4.refs_0_ = bf16[32,24,1024]{2,1,0:T(8,128)(2,1)S(1)} async-done(((bf16[32,24,1024]{2,1,0:T(8,128)(2,1)}), bf16[32,24,1024]{2,1,0:T(8,128)(2,1)S(1)}, u32[]{:S(2)}, u32[]{:S(2)}) %all-to-all-start.4) | async-done | bytes 1572896 | tf_op jit(solution)/shard_map/all_to_all | solution.py:372
  538.4 8.2 %radial.7 = (bf16[24,64,128]{2,1,0:T(8,128)(2,1)S(1)}, bf16[24,64,128]{2,1,0:T(8,128)(2,1)S(1)}, bf16[24,64,128]{2,1,0:T(8,128)(2,1)S(1)}, bf16[24,64,128]{2,1,0:T(8,128)(2,1)S(1)}) custom-call(s32[27]{0:T(128)S(1)} %pad_add_fusion.at.me, bf16[32,24,1024]{2,1,0:T(8,128)(2,1)S(1)} %all-to-all-done.4.refs_0_, s32[64,1]{1,0:T(8,128)S(1)} %copy-done.32, ...), custom_call_target="tpu_custom_call" | custom-call | flops 805306368 | bytes 15728640 | tf_op jit(solution)/shard_map/radial/pallas_call | solution.py:216
  557.3 8.4 %collective-permute-done.25.refs_3_ = bf16[24,64,128]{2,1,0:T(8,128)(2,1)S(1)} collective-permute-done((bf16[24,64,128]{2,1,0:T(8,128)(2,1)S(1)}, bf16[24,64,128]{2,1,0:T(8,128)(2,1)S(1)}, u32[]{:S(2)}, u32[]{:S(2)}) %collective-permute-start.25) | collective-permute-done | bytes 393248 | tf_op jit(solution)/shard_map/ppermute | solution.py:25
  (164 shorter events, 136.7 us)
Async XLA Ops:
  11.9 147.6 %all-to-all-start = ((bf16[32,3,128,256]{3,2,1,0:T(8,128)(2,1)}), bf16[32,3,128,256]{3,2,1,0:T(8,128)(2,1)}, u32[]{:S(2)}, u32[]{:S(2)}) async-start(bf16[32,3,128,256]{3,2,1,0:T(8,128)(2,1)} %bitcast.44), calls=%async_computation | async-start | bytes 12582912 | tf_op jit(solution)/shard_map/all_to_all | solution.py:372
  25.5 54.0 %collective-permute-start = (bf16[3,768,256]{2,1,0:T(8,128)(2,1)}, bf16[3,768,256]{2,1,0:T(8,128)(2,1)S(1)}, u32[]{:S(2)}, u32[]{:S(2)}) collective-permute-start(bf16[3,768,256]{2,1,0:T(8,128)(2,1)} %get-tuple-element.36), channel_id=1, source_target_pairs={{0,1},{1,0},{2,3},{3,2},{4,5},{5,4},{6,7},{7,6},{8,9},{9,8},{10,11... | collective-permute-start | bytes 3538952 | tf_op jit(solution)/shard_map/ppermute | solution.py:25
  25.7 79.1 %collective-permute-start.1 = (bf16[3,768,256]{2,1,0:T(8,128)(2,1)}, bf16[3,768,256]{2,1,0:T(8,128)(2,1)S(1)}, u32[]{:S(2)}, u32[]{:S(2)}) collective-permute-start(bf16[3,768,256]{2,1,0:T(8,128)(2,1)} %get-tuple-element.37), channel_id=1, source_target_pairs={{0,2},{1,3},{2,0},{3,1},{4,6},{5,7},{6,4},{7,5},{8,10},{9,11},{10,... | collective-permute-start | bytes 3538952 | tf_op jit(solution)/shard_map/ppermute | solution.py:25
  27.3 105.1 %collective-permute-start.2 = (bf16[3,768,256]{2,1,0:T(8,128)(2,1)}, bf16[3,768,256]{2,1,0:T(8,128)(2,1)S(1)}, u32[]{:S(2)}, u32[]{:S(2)}) collective-permute-start(bf16[3,768,256]{2,1,0:T(8,128)(2,1)} %get-tuple-element.38), channel_id=1, source_target_pairs={{0,3},{1,2},{2,1},{3,0},{4,7},{5,6},{6,5},{7,4},{8,11},{9,10},{10,... | collective-permute-start | bytes 3538952 | tf_op jit(solution)/shard_map/ppermute | solution.py:25
  159.4 176.1 %all-to-all-start.1 = ((bf16[32,3,128,256]{3,2,1,0:T(8,128)(2,1)}), bf16[32,3,128,256]{3,2,1,0:T(8,128)(2,1)}, u32[]{:S(2)}, u32[]{:S(2)}) async-start(bf16[32,3,128,256]{3,2,1,0:T(8,128)(2,1)} %bitcast.45), calls=%async_computation.1 | async-start | bytes 12582912 | tf_op jit(solution)/shard_map/all_to_all | solution.py:372
  169.6 40.0 %collective-permute-start.4 = (bf16[4,24,1024]{2,1,0:T(8,128)(2,1)S(1)}, bf16[4,24,1024]{2,1,0:T(8,128)(2,1)S(1)}, u32[]{:S(2)}, u32[]{:S(2)}) collective-permute-start(bf16[4,24,1024]{2,1,0:T(8,128)(2,1)S(1)} %get-tuple-element.78), channel_id=1, source_target_pairs={{0,2},{1,3},{2,0},{3,1},{4,6},{5,7},{6,4},{7,5},{8,10},{9,11},{10,... | collective-permute-start | bytes 589832 | tf_op jit(solution)/shard_map/ppermute | solution.py:25
  171.3 42.0 %collective-permute-start.5 = (bf16[4,24,1024]{2,1,0:T(8,128)(2,1)S(1)}, bf16[4,24,1024]{2,1,0:T(8,128)(2,1)S(1)}, u32[]{:S(2)}, u32[]{:S(2)}) collective-permute-start(bf16[4,24,1024]{2,1,0:T(8,128)(2,1)S(1)} %get-tuple-element.77), channel_id=1, source_target_pairs={{0,3},{1,2},{2,1},{3,0},{4,7},{5,6},{6,5},{7,4},{8,11},{9,10},{10,... | collective-permute-start | bytes 589832 | tf_op jit(solution)/shard_map/ppermute | solution.py:25
  171.3 50.7 %collective-permute-start.6 = (bf16[4,24,1024]{2,1,0:T(8,128)(2,1)S(1)}, bf16[4,24,1024]{2,1,0:T(8,128)(2,1)S(1)}, u32[]{:S(2)}, u32[]{:S(2)}) collective-permute-start(bf16[4,24,1024]{2,1,0:T(8,128)(2,1)S(1)} %get-tuple-element.76), channel_id=1, source_target_pairs={{0,4},{1,5},{2,6},{3,7},{4,0},{5,1},{6,2},{7,3},{8,12},{9,13},{10,... | collective-permute-start | bytes 589832 | tf_op jit(solution)/shard_map/ppermute | solution.py:25
  173.0 57.0 %collective-permute-start.7 = (bf16[4,24,1024]{2,1,0:T(8,128)(2,1)S(1)}, bf16[4,24,1024]{2,1,0:T(8,128)(2,1)S(1)}, u32[]{:S(2)}, u32[]{:S(2)}) collective-permute-start(bf16[4,24,1024]{2,1,0:T(8,128)(2,1)S(1)} %get-tuple-element.75), channel_id=1, source_target_pairs={{0,5},{1,4},{2,7},{3,6},{4,1},{5,0},{6,3},{7,2},{8,13},{9,12},{10,... | collective-permute-start | bytes 589832 | tf_op jit(solution)/shard_map/ppermute | solution.py:25
  173.1 67.1 %collective-permute-start.8 = (bf16[4,24,1024]{2,1,0:T(8,128)(2,1)S(1)}, bf16[4,24,1024]{2,1,0:T(8,128)(2,1)S(1)}, u32[]{:S(2)}, u32[]{:S(2)}) collective-permute-start(bf16[4,24,1024]{2,1,0:T(8,128)(2,1)S(1)} %get-tuple-element.74), channel_id=1, source_target_pairs={{0,6},{1,7},{2,4},{3,5},{4,2},{5,3},{6,0},{7,1},{8,14},{9,15},{10,... | collective-permute-start | bytes 589832 | tf_op jit(solution)/shard_map/ppermute | solution.py:25
  244.4 88.0 %collective-permute-start.14 = (bf16[3,768,256]{2,1,0:T(8,128)(2,1)S(1)}, bf16[3,768,256]{2,1,0:T(8,128)(2,1)S(1)}, u32[]{:S(2)}, u32[]{:S(2)}) collective-permute-start(bf16[3,768,256]{2,1,0:T(8,128)(2,1)S(1)} %copy-done.35), channel_id=1, source_target_pairs={{0,1},{1,0},{2,3},{3,2},{4,5},{5,4},{6,7},{7,6},{8,9},{9,8},{10,11... | collective-permute-start | bytes 3538952 | tf_op jit(solution)/shard_map/ppermute | solution.py:25
  245.1 88.3 %collective-permute-start.15 = (bf16[3,768,256]{2,1,0:T(8,128)(2,1)S(1)}, bf16[3,768,256]{2,1,0:T(8,128)(2,1)S(1)}, u32[]{:S(2)}, u32[]{:S(2)}) collective-permute-start(bf16[3,768,256]{2,1,0:T(8,128)(2,1)S(1)} %copy-done.34), channel_id=1, source_target_pairs={{0,2},{1,3},{2,0},{3,1},{4,6},{5,7},{6,4},{7,5},{8,10},{9,11},{10,... | collective-permute-start | bytes 3538952 | tf_op jit(solution)/shard_map/ppermute | solution.py:25
  245.9 88.5 %collective-permute-start.16 = (bf16[3,768,256]{2,1,0:T(8,128)(2,1)S(1)}, bf16[3,768,256]{2,1,0:T(8,128)(2,1)S(1)}, u32[]{:S(2)}, u32[]{:S(2)}) collective-permute-start(bf16[3,768,256]{2,1,0:T(8,128)(2,1)S(1)} %copy-done.33), channel_id=1, source_target_pairs={{0,3},{1,2},{2,1},{3,0},{4,7},{5,6},{6,5},{7,4},{8,11},{9,10},{10,... | collective-permute-start | bytes 3538952 | tf_op jit(solution)/shard_map/ppermute | solution.py:25
  247.7 83.2 %collective-permute-start.11 = (bf16[8,24,1024]{2,1,0:T(8,128)(2,1)S(1)}, bf16[8,24,1024]{2,1,0:T(8,128)(2,1)S(1)}, u32[]{:S(2)}, u32[]{:S(2)}) collective-permute-start(bf16[8,24,1024]{2,1,0:T(8,128)(2,1)S(1)} %get-tuple-element.41), channel_id=1, source_target_pairs={{0,16},{8,24},{16,0},{24,8},{1,17},{9,25},{17,1},{25,9},{2,18},{10... | collective-permute-start | bytes 1179656 | tf_op jit(solution)/shard_map/ppermute | solution.py:25
  277.2 54.4 %collective-permute-start.12 = (bf16[8,24,1024]{2,1,0:T(8,128)(2,1)S(1)}, bf16[8,24,1024]{2,1,0:T(8,128)(2,1)S(1)}, u32[]{:S(2)}, u32[]{:S(2)}) collective-permute-start(bf16[8,24,1024]{2,1,0:T(8,128)(2,1)S(1)} %get-tuple-element.42), channel_id=1, source_target_pairs={{0,24},{8,16},{16,8},{24,0},{1,25},{9,17},{17,9},{25,1},{2,26},{10... | collective-permute-start | bytes 1179656 | tf_op jit(solution)/shard_map/ppermute | solution.py:25
  335.5 83.7 %all-to-all-start.2 = ((bf16[32,24,2048]{2,1,0:T(8,128)(2,1)}), bf16[32,24,2048]{2,1,0:T(8,128)(2,1)}, u32[]{:S(2)}, u32[]{:S(2)}) async-start(bf16[32,24,2048]{2,1,0:T(8,128)(2,1)} %bitcast.46), calls=%async_computation.2 | async-start | bytes 6291456 | tf_op jit(solution)/shard_map/all_to_all | solution.py:372
  358.3 37.9 %collective-permute-start.19 = (bf16[24,64,128]{2,1,0:T(8,128)(2,1)S(1)}, bf16[24,64,128]{2,1,0:T(8,128)(2,1)S(1)}, u32[]{:S(2)}, u32[]{:S(2)}) collective-permute-start(bf16[24,64,128]{2,1,0:T(8,128)(2,1)S(1)} %get-tuple-element.52), channel_id=1, source_target_pairs={{0,2},{1,3},{2,0},{3,1},{4,6},{5,7},{6,4},{7,5},{8,10},{9,11},{10,... | collective-permute-start | bytes 1179656 | tf_op jit(solution)/shard_map/ppermute | solution.py:25
  419.2 76.4 %all-to-all-start.3 = ((bf16[32,24,2048]{2,1,0:T(8,128)(2,1)}), bf16[32,24,2048]{2,1,0:T(8,128)(2,1)}, u32[]{:S(2)}, u32[]{:S(2)}) async-start(bf16[32,24,2048]{2,1,0:T(8,128)(2,1)} %bitcast.47), calls=%async_computation.3 | async-start | bytes 6291456 | tf_op jit(solution)/shard_map/all_to_all | solution.py:372
  433.9 38.6 %collective-permute-start.17 = (bf16[24,128,128]{2,1,0:T(8,128)(2,1)S(1)}, bf16[24,128,128]{2,1,0:T(8,128)(2,1)S(1)}, u32[]{:S(2)}, u32[]{:S(2)}) collective-permute-start(bf16[24,128,128]{2,1,0:T(8,128)(2,1)S(1)} %get-tuple-element.49), channel_id=1, source_target_pairs={{0,3},{1,2},{2,1},{3,0},{4,7},{5,6},{6,5},{7,4},{8,11},{9,10},{10,... | collective-permute-start | bytes 2359304 | tf_op jit(solution)/shard_map/ppermute | solution.py:25
  435.2 37.3 %collective-permute-start.21 = (bf16[24,128,128]{2,1,0:T(8,128)(2,1)S(1)}, bf16[24,128,128]{2,1,0:T(8,128)(2,1)S(1)}, u32[]{:S(2)}, u32[]{:S(2)}) collective-permute-start(bf16[24,128,128]{2,1,0:T(8,128)(2,1)S(1)} %get-tuple-element.59), channel_id=1, source_target_pairs={{0,1},{1,0},{2,3},{3,2},{4,5},{5,4},{6,7},{7,6},{8,9},{9,8},{10,11... | collective-permute-start | bytes 2359304 | tf_op jit(solution)/shard_map/ppermute | solution.py:25
  435.6 59.0 %collective-permute-start.22 = (bf16[24,128,128]{2,1,0:T(8,128)(2,1)S(1)}, bf16[24,128,128]{2,1,0:T(8,128)(2,1)S(1)}, u32[]{:S(2)}, u32[]{:S(2)}) collective-permute-start(bf16[24,128,128]{2,1,0:T(8,128)(2,1)S(1)} %get-tuple-element.60), channel_id=1, source_target_pairs={{0,2},{1,3},{2,0},{3,1},{4,6},{5,7},{6,4},{7,5},{8,10},{9,11},{10,... | collective-permute-start | bytes 2359304 | tf_op jit(solution)/shard_map/ppermute | solution.py:25
  495.6 42.0 %all-to-all-start.4 = ((bf16[32,24,1024]{2,1,0:T(8,128)(2,1)}), bf16[32,24,1024]{2,1,0:T(8,128)(2,1)S(1)}, u32[]{:S(2)}, u32[]{:S(2)}) async-start(bf16[32,24,1024]{2,1,0:T(8,128)(2,1)} %bitcast.23), calls=%async_computation.4 | async-start | bytes 3145728 | tf_op jit(solution)/shard_map/all_to_all | solution.py:372
  513.0 44.3 %collective-permute-start.24 = (bf16[24,128,128]{2,1,0:T(8,128)(2,1)}, bf16[24,128,128]{2,1,0:T(8,128)(2,1)}, u32[]{:S(2)}, u32[]{:S(2)}) collective-permute-start(bf16[24,128,128]{2,1,0:T(8,128)(2,1)} %get-tuple-element.57), channel_id=1, source_target_pairs={{0,2},{1,3},{2,0},{3,1},{4,6},{5,7},{6,4},{7,5},{8,10},{9,11},{10,... | collective-permute-start | bytes 2359304 | tf_op jit(solution)/shard_map/ppermute | solution.py:25
  514.7 56.1 %collective-permute-start.20 = (bf16[24,128,128]{2,1,0:T(8,128)(2,1)}, bf16[24,128,128]{2,1,0:T(8,128)(2,1)}, u32[]{:S(2)}, u32[]{:S(2)}) collective-permute-start(bf16[24,128,128]{2,1,0:T(8,128)(2,1)} %get-tuple-element.54), channel_id=1, source_target_pairs={{0,3},{1,2},{2,1},{3,0},{4,7},{5,6},{6,5},{7,4},{8,11},{9,10},{10,... | collective-permute-start | bytes 2359304 | tf_op jit(solution)/shard_map/ppermute | solution.py:25
  (49 other events, 717.7 us)

commit v4 on v3

--- a/solution.py
+++ b/solution.py
@@ -258,7 +258,7 @@
 def put_in_order(me, pieces, place, distance, so_far, groups, width):
     rows = pieces[0].shape[0]
     columns = place.shape[2]
-    step = 8 if rows % 8 == 0 else rows
+    step = rows // math.gcd(rows, 2)
     specs = [pl.BlockSpec((step, *p.shape[1:]), lambda t, me: (t, 0, 0)) for p in pieces]
     specs.append(pl.BlockSpec(place.shape, lambda t, me: (0, 0, 0)))
     operands = list(pieces) + [place]
@@ -291,20 +291,22 @@
     here = xs[0].shape[0] * len(xs)
     shell_blocks, sharers, _, columns = out.shape[:4]
     depth = xs[0].shape[2] * HALF
-    for g in range(0, here, 2 * HALF):
-        x, start = xs[g * len(xs) // here], g % (here // len(xs))
-        found = [
-            jnp.dot(
-                pick[...],
-                x[start + h : start + h + HALF, 0].reshape(depth, x.shape[3]),
-                preferred_element_type=jnp.float32,
-            )
-            for h in (0, HALF)
-        ]
-        for n in range(shell_blocks * sharers * columns):
-            rows = jnp.concatenate([f[n * HALF : (n + 1) * HALF] for f in found], axis=0)
-            block, rest = divmod(n, sharers * columns)
-            out[block, rest // columns, 0, rest % columns, 0, g : g + 2 * HALF] = rows.astype(out.dtype)
+    parts = out.shape[4]
+    for c in range(xs[0].shape[1]):
+        for g in range(0, here, 2 * HALF):
+            x, start = xs[g * len(xs) // here], g % (here // len(xs))
+            found = [
+                jnp.dot(
+                    pick[...],
+                    x[start + h : start + h + HALF, c].reshape(depth, x.shape[3]),
+                    preferred_element_type=jnp.float32,
+                )
+                for h in (0, HALF)
+            ]
+            for n in range(shell_blocks * sharers * columns):
+                rows = jnp.concatenate([f[n * HALF : (n + 1) * HALF] for f in found], axis=0)
+                block, rest = divmod(n, sharers * columns)
+                out[block, rest // columns, c // parts, rest % columns, c % parts, g : g + 2 * HALF] = rows.astype(out.dtype)
 
 
 def pack(x, span, shells, sharers, spread):
@@ -321,16 +323,16 @@
     slices = math.gcd(here // (2 * HALF), 4)
     return pl.pallas_call(
         pack_kernel,
-        grid=(shells // together, complex_parts),
+        grid=(shells // together,),
         in_specs=[
             *[
-                pl.BlockSpec((here // slices, 1, together * local, cycles), lambda b, c, q=q: (q, c, b, 0))
+                pl.BlockSpec((here // slices, complex_parts, together * local, cycles), lambda b, q=q: (q, 0, b, 0))
                 for q in range(slices)
             ],
-            pl.BlockSpec(pick.shape, lambda b, c: (0, 0)),
+            pl.BlockSpec(pick.shape, lambda b: (0, 0)),
         ],
         out_specs=pl.BlockSpec(
-            (together, sharers, 1, columns, 1, here, cycles), lambda b, c: (b, 0, c // parts, 0, c % parts, 0, 0)
+            (together, sharers, spread, columns, parts, here, cycles), lambda b: (b, 0, 0, 0, 0, 0, 0)
         ),
         out_shape=jax.ShapeDtypeStruct(shape, jnp.bfloat16),
         compiler_params=pltpu.CompilerParams(vmem_limit_bytes=VMEM),

time: 580 us -> 578 us (level)
  Pallas kernels: 125 us -> 119 us
  transfers between devices with their start and end apart: 33 -> 33, of which waited for: 20 -> 20; matrix products, arithmetic and copies ran while one was open for 4% -> 4% of each run, Pallas kernels for 19% -> 18%
where the time goes in v4:
time: 578 us; the launch traced here: 576 us
  waiting for transfers between devices  361 us (62%)
  Pallas kernels  119 us (21%)
  starting transfers between devices  57.8 us (10%)
  local copies, waits for them, and re-layouts  36.9 us (6%)
    ppermute x28, waiting for transfers between devices, exchange(): lax.ppermute(blocks[d], axis, [(i, i ^ d) for i in range(size)])  288 us
    all_to_all x5, waiting for transfers between devices, move(): return lax.all_to_all(x, axes, split_axis=0, concat_axis=0, tiled=True)  72.6 us
    pallas_call x4, Pallas kernels, radial_transform(): pl.pallas_call(functools.partial(radial_kernel, groups, far, step, slices...  36 us
    all_to_all x5, starting transfers between devices, move(): return lax.all_to_all(x, axes, split_axis=0, concat_axis=0, tiled=True)  34.3 us
    pallas_call x4, Pallas kernels, legendre_transform(): pl.pallas_call(functools.partial(legendre_kernel, groups, parts, by_dista...  23.6 us
    ppermute x28, starting transfers between devices, exchange(): lax.ppermute(blocks[d], axis, [(i, i ^ d) for i in range(size)])  23.5 us
    pallas_call x1, Pallas kernels, radial_filter(): pl.pallas_call(functools.partial(filter_kernel, groups), grid_spec=pltpu....  23.4 us
    pallas_call x2, Pallas kernels, pack(): pl.pallas_call(pack_kernel, grid=(shells // together,), in_specs=[*[pl.Bl...  18.1 us
  transfers between devices with their start and end apart: 33, of which 20 were waited for; matrix products, arithmetic and copies ran while one was open for 4% of the time, Pallas kernels for 18%

profile of v4, /device:TPU:0, one launch (start us, length us, event | category | flops | bytes accessed | tf_op | source)
XLA Modules:
  0.0 575.9 jit_solution(12517051672728653585)
XLA Ops:
  0.9 9.0 %pack.2 = bf16[8,4,1,3,2,64,256]{6,5,4,3,2,1,0:T(8,128)(2,1)} custom-call(bf16[64,2,192,256]{3,2,1,0:T(8,128)(2,1)} %refs_3_.3, bf16[64,2,192,256]{3,2,1,0:T(8,128)(2,1)} %refs_3_.3, bf16[64,2,192,256]{3,2,1,0:T(8,128)(2,1)} %refs_3_.3, bf16[64,2,192,256]{3,2,1,0:T(8,128)(2,1)} %refs_3_.3, bf16[192,384]{1,0:T(8,128)(2,1)S(1)} %copy-done.31), custom_call_target="tpu_custom_call" | custom-call | flops 2415919104 | bytes 18874368 | tf_op jit(solution)/shard_map/pack/pallas_call | solution.py:324
  43.0 9.1 %pack.3 = bf16[8,4,1,3,2,64,256]{6,5,4,3,2,1,0:T(8,128)(2,1)} custom-call(bf16[64,2,192,256]{3,2,1,0:T(8,128)(2,1)} %refs_3_.3, bf16[64,2,192,256]{3,2,1,0:T(8,128)(2,1)} %refs_3_.3, bf16[64,2,192,256]{3,2,1,0:T(8,128)(2,1)} %refs_3_.3, bf16[64,2,192,256]{3,2,1,0:T(8,128)(2,1)} %refs_3_.3, bf16[192,384]{1,0:T(8,128)(2,1)S(1)} %copy-done.30), custom_call_target="tpu_custom_call" | custom-call | flops 2415919104 | bytes 18874368 | tf_op jit(solution)/shard_map/pack/pallas_call | solution.py:324
  52.1 23.4 %radial_filter.1.refs_5_.refs_6_.refs_7_.refs_8_.refs_2_.refs_3_.refs_4_ = bf16[24,512,512]{2,1,0:T(8,128)(2,1)} custom-call(s32[27]{0:T(128)S(1)} %pad_add_fusion.at.me, bf16[24,512,512]{2,1,0:T(8,128)(2,1)} %bessel.1, f32[24,1,512]{2,1,0:T(1,128)S(1)} %copy-done.28, f32[24,1,512]{2,1,0:T(1,128)S(1)} %copy-done.29), custom_call_target="tpu_custom_call" | custom-call | flops 6442450944 | bytes 25165824 | tf_op jit(solution)/shard_map/radial_filter/pallas_call | solution.py:126
  75.5 27.3 %collective-permute-done.1.refs_1_ = bf16[3,768,256]{2,1,0:T(8,128)(2,1)S(1)} collective-permute-done((bf16[3,768,256]{2,1,0:T(8,128)(2,1)}, bf16[3,768,256]{2,1,0:T(8,128)(2,1)S(1)}, u32[]{:S(2)}, u32[]{:S(2)}) %collective-permute-start.1) | collective-permute-done | bytes 1179680 | tf_op jit(solution)/shard_map/ppermute | solution.py:25
  102.8 27.8 %collective-permute-done.2.refs_2_ = bf16[3,768,256]{2,1,0:T(8,128)(2,1)S(1)} collective-permute-done((bf16[3,768,256]{2,1,0:T(8,128)(2,1)}, bf16[3,768,256]{2,1,0:T(8,128)(2,1)S(1)}, u32[]{:S(2)}, u32[]{:S(2)}) %collective-permute-start.2) | collective-permute-done | bytes 1179680 | tf_op jit(solution)/shard_map/ppermute | solution.py:25
  130.6 26.9 %all-to-all-done = bf16[32,3,128,256]{3,2,1,0:T(8,128)(2,1)} async-done(((bf16[32,3,128,256]{3,2,1,0:T(8,128)(2,1)}), bf16[32,3,128,256]{3,2,1,0:T(8,128)(2,1)}, u32[]{:S(2)}, u32[]{:S(2)}) %all-to-all-start) | async-done | bytes 6291488 | tf_op jit(solution)/shard_map/all_to_all | solution.py:374
  173.7 33.9 %collective-permute-done.4.refs_2_ = bf16[4,24,1024]{2,1,0:T(8,128)(2,1)S(1)} collective-permute-done((bf16[4,24,1024]{2,1,0:T(8,128)(2,1)S(1)}, bf16[4,24,1024]{2,1,0:T(8,128)(2,1)S(1)}, u32[]{:S(2)}, u32[]{:S(2)}) %collective-permute-start.4) | collective-permute-done | bytes 196640 | tf_op jit(solution)/shard_map/ppermute | solution.py:25
  211.4 8.7 %collective-permute-done.6.refs_4_ = bf16[4,24,1024]{2,1,0:T(8,128)(2,1)S(1)} collective-permute-done((bf16[4,24,1024]{2,1,0:T(8,128)(2,1)S(1)}, bf16[4,24,1024]{2,1,0:T(8,128)(2,1)S(1)}, u32[]{:S(2)}, u32[]{:S(2)}) %collective-permute-start.6) | collective-permute-done | bytes 196640 | tf_op jit(solution)/shard_map/ppermute | solution.py:25
  220.1 7.9 %collective-permute-done.7.refs_5_ = bf16[4,24,1024]{2,1,0:T(8,128)(2,1)S(1)} collective-permute-done((bf16[4,24,1024]{2,1,0:T(8,128)(2,1)S(1)}, bf16[4,24,1024]{2,1,0:T(8,128)(2,1)S(1)}, u32[]{:S(2)}, u32[]{:S(2)}) %collective-permute-start.7) | collective-permute-done | bytes 196640 | tf_op jit(solution)/shard_map/ppermute | solution.py:25
  228.0 10.3 %collective-permute-done.8.refs_6_ = bf16[4,24,1024]{2,1,0:T(8,128)(2,1)S(1)} collective-permute-done((bf16[4,24,1024]{2,1,0:T(8,128)(2,1)S(1)}, bf16[4,24,1024]{2,1,0:T(8,128)(2,1)S(1)}, u32[]{:S(2)}, u32[]{:S(2)}) %collective-permute-start.8) | collective-permute-done | bytes 196640 | tf_op jit(solution)/shard_map/ppermute | solution.py:25
  245.8 29.5 %collective-permute-done.10.refs_1_ = bf16[8,24,1024]{2,1,0:T(8,128)(2,1)S(1)} collective-permute-done((bf16[8,24,1024]{2,1,0:T(8,128)(2,1)S(1)}, bf16[8,24,1024]{2,1,0:T(8,128)(2,1)S(1)}, u32[]{:S(2)}, u32[]{:S(2)}) %collective-permute-start.10) | collective-permute-done | bytes 393248 | tf_op jit(solution)/shard_map/ppermute | solution.py:25
  285.7 43.2 %collective-permute-done.11.refs_2_ = bf16[8,24,1024]{2,1,0:T(8,128)(2,1)S(1)} collective-permute-done((bf16[8,24,1024]{2,1,0:T(8,128)(2,1)S(1)}, bf16[8,24,1024]{2,1,0:T(8,128)(2,1)S(1)}, u32[]{:S(2)}, u32[]{:S(2)}) %collective-permute-start.11) | collective-permute-done | bytes 393248 | tf_op jit(solution)/shard_map/ppermute | solution.py:25
  333.6 12.2 %all-to-all-start.2 = ((bf16[32,24,2048]{2,1,0:T(8,128)(2,1)}), bf16[32,24,2048]{2,1,0:T(8,128)(2,1)}, u32[]{:S(2)}, u32[]{:S(2)}) async-start(bf16[32,24,2048]{2,1,0:T(8,128)(2,1)} %bitcast.46), calls=%async_computation.2 | async-start | bytes 6291456 | tf_op jit(solution)/shard_map/all_to_all | solution.py:374
  346.0 8.7 %radial.4 = (bf16[24,64,128]{2,1,0:T(8,128)(2,1)S(1)}, bf16[24,64,128]{2,1,0:T(8,128)(2,1)S(1)}, bf16[24,64,128]{2,1,0:T(8,128)(2,1)S(1)}, bf16[24,64,128]{2,1,0:T(8,128)(2,1)S(1)}) custom-call(s32[27]{0:T(128)S(1)} %pad_add_fusion.at.me, bf16[8,24,1024]{2,1,0:T(8,128)(2,1)S(1)} %copy-done.14, bf16[8,24,1024]{2,1,0:T(8,128)(2,1)S(1)} %copy-done.16, ...), custom_call_target="tpu_custom_call" | custom-call | flops 805306368 | bytes 15728640 | tf_op jit(solution)/shard_map/radial/pallas_call | solution.py:216
  369.3 15.5 %collective-permute-done.13.refs_0_ = bf16[24,64,128]{2,1,0:T(8,128)(2,1)S(1)} collective-permute-done((bf16[24,64,128]{2,1,0:T(8,128)(2,1)S(1)}, bf16[24,64,128]{2,1,0:T(8,128)(2,1)S(1)}, u32[]{:S(2)}, u32[]{:S(2)}) %collective-permute-start.13) | collective-permute-done | bytes 393248 | tf_op jit(solution)/shard_map/ppermute | solution.py:25
  386.3 7.9 %collective-permute-done.19.refs_0_ = bf16[24,64,128]{2,1,0:T(8,128)(2,1)S(1)} collective-permute-done((bf16[24,64,128]{2,1,0:T(8,128)(2,1)S(1)}, bf16[24,64,128]{2,1,0:T(8,128)(2,1)S(1)}, u32[]{:S(2)}, u32[]{:S(2)}) %collective-permute-start.19) | collective-permute-done | bytes 393248 | tf_op jit(solution)/shard_map/ppermute | solution.py:25
  395.0 22.4 %all-to-all-done.2.refs_0_ = bf16[32,24,2048]{2,1,0:T(8,128)(2,1)} async-done(((bf16[32,24,2048]{2,1,0:T(8,128)(2,1)}), bf16[32,24,2048]{2,1,0:T(8,128)(2,1)}, u32[]{:S(2)}, u32[]{:S(2)}) %all-to-all-start.2) | async-done | bytes 3145760 | tf_op jit(solution)/shard_map/all_to_all | solution.py:374
  422.1 8.9 %radial.5 = (bf16[24,128,128]{2,1,0:T(8,128)(2,1)S(1)}, bf16[24,128,128]{2,1,0:T(8,128)(2,1)S(1)}, bf16[24,128,128]{2,1,0:T(8,128)(2,1)S(1)}, bf16[24,128,128]{2,1,0:T(8,128)(2,1)S(1)}) custom-call(s32[27]{0:T(128)S(1)} %pad_add_fusion.at.me, bf16[32,24,2048]{2,1,0:T(8,128)(2,1)} %all-to-all-done.2.refs_0_, s32[128,1]{1,0:T(8,128)S(1)} %copy.31.refs_1_, ...), custom_call_target="tpu_custom_call" | custom-call | flops 1610612736 | bytes 18874368 | tf_op jit(solution)/shard_map/radial/pallas_call | solution.py:216
  434.0 36.6 %collective-permute-done.17.refs_1_ = bf16[24,128,128]{2,1,0:T(8,128)(2,1)S(1)} collective-permute-done((bf16[24,128,128]{2,1,0:T(8,128)(2,1)S(1)}, bf16[24,128,128]{2,1,0:T(8,128)(2,1)S(1)}, u32[]{:S(2)}, u32[]{:S(2)}) %collective-permute-start.17) | collective-permute-done | bytes 786464 | tf_op jit(solution)/shard_map/ppermute | solution.py:25
  471.5 21.2 %collective-permute-done.22.refs_1_ = bf16[24,128,128]{2,1,0:T(8,128)(2,1)S(1)} collective-permute-done((bf16[24,128,128]{2,1,0:T(8,128)(2,1)S(1)}, bf16[24,128,128]{2,1,0:T(8,128)(2,1)S(1)}, u32[]{:S(2)}, u32[]{:S(2)}) %collective-permute-start.22) | collective-permute-done | bytes 786464 | tf_op jit(solution)/shard_map/ppermute | solution.py:25
  499.8 10.2 %radial.6 = (bf16[24,128,128]{2,1,0:T(8,128)(2,1)S(1)}, bf16[24,128,128]{2,1,0:T(8,128)(2,1)}, bf16[24,128,128]{2,1,0:T(8,128)(2,1)}, bf16[24,128,128]{2,1,0:T(8,128)(2,1)}) custom-call(s32[27]{0:T(128)S(1)} %pad_add_fusion.at.me, bf16[32,24,2048]{2,1,0:T(8,128)(2,1)} %all-to-all-done.3.refs_0_, s32[128,1]{1,0:T(8,128)S(1)} %copy-done.27, ...), custom_call_target="tpu_custom_call" | custom-call | flops 1610612736 | bytes 18874368 | tf_op jit(solution)/shard_map/radial/pallas_call | solution.py:216
  513.5 22.2 %all-to-all-done.4.refs_0_ = bf16[32,24,1024]{2,1,0:T(8,128)(2,1)S(1)} async-done(((bf16[32,24,1024]{2,1,0:T(8,128)(2,1)}), bf16[32,24,1024]{2,1,0:T(8,128)(2,1)S(1)}, u32[]{:S(2)}, u32[]{:S(2)}) %all-to-all-start.4) | async-done | bytes 1572896 | tf_op jit(solution)/shard_map/all_to_all | solution.py:374
  536.5 8.2 %radial.7 = (bf16[24,64,128]{2,1,0:T(8,128)(2,1)S(1)}, bf16[24,64,128]{2,1,0:T(8,128)(2,1)S(1)}, bf16[24,64,128]{2,1,0:T(8,128)(2,1)S(1)}, bf16[24,64,128]{2,1,0:T(8,128)(2,1)S(1)}) custom-call(s32[27]{0:T(128)S(1)} %pad_add_fusion.at.me, bf16[32,24,1024]{2,1,0:T(8,128)(2,1)S(1)} %all-to-all-done.4.refs_0_, s32[64,1]{1,0:T(8,128)S(1)} %copy-done.32, ...), custom_call_target="tpu_custom_call" | custom-call | flops 805306368 | bytes 15728640 | tf_op jit(solution)/shard_map/radial/pallas_call | solution.py:216
  554.8 9.0 %collective-permute-done.25.refs_3_ = bf16[24,64,128]{2,1,0:T(8,128)(2,1)S(1)} collective-permute-done((bf16[24,64,128]{2,1,0:T(8,128)(2,1)S(1)}, bf16[24,64,128]{2,1,0:T(8,128)(2,1)S(1)}, u32[]{:S(2)}, u32[]{:S(2)}) %collective-permute-start.25) | collective-permute-done | bytes 393248 | tf_op jit(solution)/shard_map/ppermute | solution.py:25
  (164 shorter events, 135.6 us)
Async XLA Ops:
  9.9 147.6 %all-to-all-start = ((bf16[32,3,128,256]{3,2,1,0:T(8,128)(2,1)}), bf16[32,3,128,256]{3,2,1,0:T(8,128)(2,1)}, u32[]{:S(2)}, u32[]{:S(2)}) async-start(bf16[32,3,128,256]{3,2,1,0:T(8,128)(2,1)} %bitcast.44), calls=%async_computation | async-start | bytes 12582912 | tf_op jit(solution)/shard_map/all_to_all | solution.py:374
  23.6 52.0 %collective-permute-start = (bf16[3,768,256]{2,1,0:T(8,128)(2,1)}, bf16[3,768,256]{2,1,0:T(8,128)(2,1)S(1)}, u32[]{:S(2)}, u32[]{:S(2)}) collective-permute-start(bf16[3,768,256]{2,1,0:T(8,128)(2,1)} %get-tuple-element.36), channel_id=1, source_target_pairs={{0,1},{1,0},{2,3},{3,2},{4,5},{5,4},{6,7},{7,6},{8,9},{9,8},{10,11... | collective-permute-start | bytes 3538952 | tf_op jit(solution)/shard_map/ppermute | solution.py:25
  23.7 79.1 %collective-permute-start.1 = (bf16[3,768,256]{2,1,0:T(8,128)(2,1)}, bf16[3,768,256]{2,1,0:T(8,128)(2,1)S(1)}, u32[]{:S(2)}, u32[]{:S(2)}) collective-permute-start(bf16[3,768,256]{2,1,0:T(8,128)(2,1)} %get-tuple-element.37), channel_id=1, source_target_pairs={{0,2},{1,3},{2,0},{3,1},{4,6},{5,7},{6,4},{7,5},{8,10},{9,11},{10,... | collective-permute-start | bytes 3538952 | tf_op jit(solution)/shard_map/ppermute | solution.py:25
  25.4 105.1 %collective-permute-start.2 = (bf16[3,768,256]{2,1,0:T(8,128)(2,1)}, bf16[3,768,256]{2,1,0:T(8,128)(2,1)S(1)}, u32[]{:S(2)}, u32[]{:S(2)}) collective-permute-start(bf16[3,768,256]{2,1,0:T(8,128)(2,1)} %get-tuple-element.38), channel_id=1, source_target_pairs={{0,3},{1,2},{2,1},{3,0},{4,7},{5,6},{6,5},{7,4},{8,11},{9,10},{10,... | collective-permute-start | bytes 3538952 | tf_op jit(solution)/shard_map/ppermute | solution.py:25
  157.5 176.1 %all-to-all-start.1 = ((bf16[32,3,128,256]{3,2,1,0:T(8,128)(2,1)}), bf16[32,3,128,256]{3,2,1,0:T(8,128)(2,1)}, u32[]{:S(2)}, u32[]{:S(2)}) async-start(bf16[32,3,128,256]{3,2,1,0:T(8,128)(2,1)} %bitcast.45), calls=%async_computation.1 | async-start | bytes 12582912 | tf_op jit(solution)/shard_map/all_to_all | solution.py:374
  167.7 40.0 %collective-permute-start.4 = (bf16[4,24,1024]{2,1,0:T(8,128)(2,1)S(1)}, bf16[4,24,1024]{2,1,0:T(8,128)(2,1)S(1)}, u32[]{:S(2)}, u32[]{:S(2)}) collective-permute-start(bf16[4,24,1024]{2,1,0:T(8,128)(2,1)S(1)} %get-tuple-element.78), channel_id=1, source_target_pairs={{0,2},{1,3},{2,0},{3,1},{4,6},{5,7},{6,4},{7,5},{8,10},{9,11},{10,... | collective-permute-start | bytes 589832 | tf_op jit(solution)/shard_map/ppermute | solution.py:25
  169.3 42.0 %collective-permute-start.5 = (bf16[4,24,1024]{2,1,0:T(8,128)(2,1)S(1)}, bf16[4,24,1024]{2,1,0:T(8,128)(2,1)S(1)}, u32[]{:S(2)}, u32[]{:S(2)}) collective-permute-start(bf16[4,24,1024]{2,1,0:T(8,128)(2,1)S(1)} %get-tuple-element.77), channel_id=1, source_target_pairs={{0,3},{1,2},{2,1},{3,0},{4,7},{5,6},{6,5},{7,4},{8,11},{9,10},{10,... | collective-permute-start | bytes 589832 | tf_op jit(solution)/shard_map/ppermute | solution.py:25
  169.4 50.7 %collective-permute-start.6 = (bf16[4,24,1024]{2,1,0:T(8,128)(2,1)S(1)}, bf16[4,24,1024]{2,1,0:T(8,128)(2,1)S(1)}, u32[]{:S(2)}, u32[]{:S(2)}) collective-permute-start(bf16[4,24,1024]{2,1,0:T(8,128)(2,1)S(1)} %get-tuple-element.76), channel_id=1, source_target_pairs={{0,4},{1,5},{2,6},{3,7},{4,0},{5,1},{6,2},{7,3},{8,12},{9,13},{10,... | collective-permute-start | bytes 589832 | tf_op jit(solution)/shard_map/ppermute | solution.py:25
  171.0 56.9 %collective-permute-start.7 = (bf16[4,24,1024]{2,1,0:T(8,128)(2,1)S(1)}, bf16[4,24,1024]{2,1,0:T(8,128)(2,1)S(1)}, u32[]{:S(2)}, u32[]{:S(2)}) collective-permute-start(bf16[4,24,1024]{2,1,0:T(8,128)(2,1)S(1)} %get-tuple-element.75), channel_id=1, source_target_pairs={{0,5},{1,4},{2,7},{3,6},{4,1},{5,0},{6,3},{7,2},{8,13},{9,12},{10,... | collective-permute-start | bytes 589832 | tf_op jit(solution)/shard_map/ppermute | solution.py:25
  171.2 67.1 %collective-permute-start.8 = (bf16[4,24,1024]{2,1,0:T(8,128)(2,1)S(1)}, bf16[4,24,1024]{2,1,0:T(8,128)(2,1)S(1)}, u32[]{:S(2)}, u32[]{:S(2)}) collective-permute-start(bf16[4,24,1024]{2,1,0:T(8,128)(2,1)S(1)} %get-tuple-element.74), channel_id=1, source_target_pairs={{0,6},{1,7},{2,4},{3,5},{4,2},{5,3},{6,0},{7,1},{8,14},{9,15},{10,... | collective-permute-start | bytes 589832 | tf_op jit(solution)/shard_map/ppermute | solution.py:25
  242.5 88.0 %collective-permute-start.14 = (bf16[3,768,256]{2,1,0:T(8,128)(2,1)S(1)}, bf16[3,768,256]{2,1,0:T(8,128)(2,1)S(1)}, u32[]{:S(2)}, u32[]{:S(2)}) collective-permute-start(bf16[3,768,256]{2,1,0:T(8,128)(2,1)S(1)} %copy-done.35), channel_id=1, source_target_pairs={{0,1},{1,0},{2,3},{3,2},{4,5},{5,4},{6,7},{7,6},{8,9},{9,8},{10,11... | collective-permute-start | bytes 3538952 | tf_op jit(solution)/shard_map/ppermute | solution.py:25
  243.1 88.3 %collective-permute-start.15 = (bf16[3,768,256]{2,1,0:T(8,128)(2,1)S(1)}, bf16[3,768,256]{2,1,0:T(8,128)(2,1)S(1)}, u32[]{:S(2)}, u32[]{:S(2)}) collective-permute-start(bf16[3,768,256]{2,1,0:T(8,128)(2,1)S(1)} %copy-done.34), channel_id=1, source_target_pairs={{0,2},{1,3},{2,0},{3,1},{4,6},{5,7},{6,4},{7,5},{8,10},{9,11},{10,... | collective-permute-start | bytes 3538952 | tf_op jit(solution)/shard_map/ppermute | solution.py:25
  244.0 88.5 %collective-permute-start.16 = (bf16[3,768,256]{2,1,0:T(8,128)(2,1)S(1)}, bf16[3,768,256]{2,1,0:T(8,128)(2,1)S(1)}, u32[]{:S(2)}, u32[]{:S(2)}) collective-permute-start(bf16[3,768,256]{2,1,0:T(8,128)(2,1)S(1)} %copy-done.33), channel_id=1, source_target_pairs={{0,3},{1,2},{2,1},{3,0},{4,7},{5,6},{6,5},{7,4},{8,11},{9,10},{10,... | collective-permute-start | bytes 3538952 | tf_op jit(solution)/shard_map/ppermute | solution.py:25
  245.8 83.2 %collective-permute-start.11 = (bf16[8,24,1024]{2,1,0:T(8,128)(2,1)S(1)}, bf16[8,24,1024]{2,1,0:T(8,128)(2,1)S(1)}, u32[]{:S(2)}, u32[]{:S(2)}) collective-permute-start(bf16[8,24,1024]{2,1,0:T(8,128)(2,1)S(1)} %get-tuple-element.41), channel_id=1, source_target_pairs={{0,16},{8,24},{16,0},{24,8},{1,17},{9,25},{17,1},{25,9},{2,18},{10... | collective-permute-start | bytes 1179656 | tf_op jit(solution)/shard_map/ppermute | solution.py:25
  275.3 54.4 %collective-permute-start.12 = (bf16[8,24,1024]{2,1,0:T(8,128)(2,1)S(1)}, bf16[8,24,1024]{2,1,0:T(8,128)(2,1)S(1)}, u32[]{:S(2)}, u32[]{:S(2)}) collective-permute-start(bf16[8,24,1024]{2,1,0:T(8,128)(2,1)S(1)} %get-tuple-element.42), channel_id=1, source_target_pairs={{0,24},{8,16},{16,8},{24,0},{1,25},{9,17},{17,9},{25,1},{2,26},{10... | collective-permute-start | bytes 1179656 | tf_op jit(solution)/shard_map/ppermute | solution.py:25
  333.6 83.7 %all-to-all-start.2 = ((bf16[32,24,2048]{2,1,0:T(8,128)(2,1)}), bf16[32,24,2048]{2,1,0:T(8,128)(2,1)}, u32[]{:S(2)}, u32[]{:S(2)}) async-start(bf16[32,24,2048]{2,1,0:T(8,128)(2,1)} %bitcast.46), calls=%async_computation.2 | async-start | bytes 6291456 | tf_op jit(solution)/shard_map/all_to_all | solution.py:374
  356.4 37.9 %collective-permute-start.19 = (bf16[24,64,128]{2,1,0:T(8,128)(2,1)S(1)}, bf16[24,64,128]{2,1,0:T(8,128)(2,1)S(1)}, u32[]{:S(2)}, u32[]{:S(2)}) collective-permute-start(bf16[24,64,128]{2,1,0:T(8,128)(2,1)S(1)} %get-tuple-element.52), channel_id=1, source_target_pairs={{0,2},{1,3},{2,0},{3,1},{4,6},{5,7},{6,4},{7,5},{8,10},{9,11},{10,... | collective-permute-start | bytes 1179656 | tf_op jit(solution)/shard_map/ppermute | solution.py:25
  417.3 76.4 %all-to-all-start.3 = ((bf16[32,24,2048]{2,1,0:T(8,128)(2,1)}), bf16[32,24,2048]{2,1,0:T(8,128)(2,1)}, u32[]{:S(2)}, u32[]{:S(2)}) async-start(bf16[32,24,2048]{2,1,0:T(8,128)(2,1)} %bitcast.47), calls=%async_computation.3 | async-start | bytes 6291456 | tf_op jit(solution)/shard_map/all_to_all | solution.py:374
  431.8 38.7 %collective-permute-start.17 = (bf16[24,128,128]{2,1,0:T(8,128)(2,1)S(1)}, bf16[24,128,128]{2,1,0:T(8,128)(2,1)S(1)}, u32[]{:S(2)}, u32[]{:S(2)}) collective-permute-start(bf16[24,128,128]{2,1,0:T(8,128)(2,1)S(1)} %get-tuple-element.49), channel_id=1, source_target_pairs={{0,3},{1,2},{2,1},{3,0},{4,7},{5,6},{6,5},{7,4},{8,11},{9,10},{10,... | collective-permute-start | bytes 2359304 | tf_op jit(solution)/shard_map/ppermute | solution.py:25
  433.3 37.3 %collective-permute-start.21 = (bf16[24,128,128]{2,1,0:T(8,128)(2,1)S(1)}, bf16[24,128,128]{2,1,0:T(8,128)(2,1)S(1)}, u32[]{:S(2)}, u32[]{:S(2)}) collective-permute-start(bf16[24,128,128]{2,1,0:T(8,128)(2,1)S(1)} %get-tuple-element.59), channel_id=1, source_target_pairs={{0,1},{1,0},{2,3},{3,2},{4,5},{5,4},{6,7},{7,6},{8,9},{9,8},{10,11... | collective-permute-start | bytes 2359304 | tf_op jit(solution)/shard_map/ppermute | solution.py:25
  433.7 59.0 %collective-permute-start.22 = (bf16[24,128,128]{2,1,0:T(8,128)(2,1)S(1)}, bf16[24,128,128]{2,1,0:T(8,128)(2,1)S(1)}, u32[]{:S(2)}, u32[]{:S(2)}) collective-permute-start(bf16[24,128,128]{2,1,0:T(8,128)(2,1)S(1)} %get-tuple-element.60), channel_id=1, source_target_pairs={{0,2},{1,3},{2,0},{3,1},{4,6},{5,7},{6,4},{7,5},{8,10},{9,11},{10,... | collective-permute-start | bytes 2359304 | tf_op jit(solution)/shard_map/ppermute | solution.py:25
  493.7 42.0 %all-to-all-start.4 = ((bf16[32,24,1024]{2,1,0:T(8,128)(2,1)}), bf16[32,24,1024]{2,1,0:T(8,128)(2,1)S(1)}, u32[]{:S(2)}, u32[]{:S(2)}) async-start(bf16[32,24,1024]{2,1,0:T(8,128)(2,1)} %bitcast.23), calls=%async_computation.4 | async-start | bytes 3145728 | tf_op jit(solution)/shard_map/all_to_all | solution.py:374
  511.1 43.7 %collective-permute-start.24 = (bf16[24,128,128]{2,1,0:T(8,128)(2,1)}, bf16[24,128,128]{2,1,0:T(8,128)(2,1)}, u32[]{:S(2)}, u32[]{:S(2)}) collective-permute-start(bf16[24,128,128]{2,1,0:T(8,128)(2,1)} %get-tuple-element.57), channel_id=1, source_target_pairs={{0,2},{1,3},{2,0},{3,1},{4,6},{5,7},{6,4},{7,5},{8,10},{9,11},{10,... | collective-permute-start | bytes 2359304 | tf_op jit(solution)/shard_map/ppermute | solution.py:25
  512.8 55.7 %collective-permute-start.20 = (bf16[24,128,128]{2,1,0:T(8,128)(2,1)}, bf16[24,128,128]{2,1,0:T(8,128)(2,1)}, u32[]{:S(2)}, u32[]{:S(2)}) collective-permute-start(bf16[24,128,128]{2,1,0:T(8,128)(2,1)} %get-tuple-element.54), channel_id=1, source_target_pairs={{0,3},{1,2},{2,1},{3,0},{4,7},{5,6},{6,5},{7,4},{8,11},{9,10},{10,... | collective-permute-start | bytes 2359304 | tf_op jit(solution)/shard_map/ppermute | solution.py:25
  (49 other events, 714.6 us)
